TPU v7x, 512 devices: a whole 4x4x16 slice. The times are simulated.
512 devices in a mesh: row: 16 (over y, x), col: 32 (over z, core).
Axes of the slice: x: 4, y: 4, z: 16, core: 2. Of those that a mesh axis runs over, the one named last changes fastest.
Arguments:
- tile_weights: bfloat16 [16, 32, 32, 128, 128], P('row', 'col'), may hold values from 0 to 4, as said below
- tile_pos: int32 [16, 32, 2, 32], P('row', 'col'), may hold values from 0 to 7, as said below
- tile_total: int32 [16, 32], P('row', 'col'), may hold values from 1 to 32, as said below
- root_ids: int32 [128], replicated, may hold values from 0 to 16383
Outputs:
- hop_level: int32 [16384, 128], P(('row', 'col'))
- path_share: float32 [16384, 128], P(('row', 'col'))
- found_per_level: float32 [4, 128], replicated
Inputs may be any that keep to these rules, and one draw needn't show every extreme that they name: `tile_weights`: nonnegative; an entry is zero wherever the tile has no edge. `tile_pos`: the slots of one device name distinct tile positions; tile rows lie below 8 and tile columns below 4. `tile_total`: some device uses all 32 slots; slots at or past a device's total hold arbitrary positions and zero weights.
All inputs are finite; a program needn't handle non-finite values.
Results may differ from a plain program's by a relative error of at most 0.01.
Values may be sent and summed in bfloat16 or wider, within the bound.
No kernel may reach another device: no remote copies, remote signals or barrier semaphores. Data moves between devices by JAX's collectives and lax.ppermute only.
A program may use at most 64 MiB of HBM per device.

v0:
```python
import jax
import jax.numpy as jnp
from jax import lax
from jax.sharding import Mesh
from jax.sharding import PartitionSpec as P

ROOTS = 128
PV = 32
LEVELS = 4
COL = ("col_0", "col_1")
ROW = ("row_0", "row_1")
ROW_COL = ("row_0", "row_1", "col_0", "col_1")


def sent_to_all(shard, axis):
    devices = lax.axis_size(axis)
    return lax.all_to_all(
        jnp.broadcast_to(shard[None], (devices, *shard.shape)), axis, 0, 0, tiled=True
    )


def joined_along(tiles, dim):
    tiles = jnp.moveaxis(tiles, 0, dim)
    shape = tiles.shape
    return tiles.reshape(*shape[:dim], shape[dim] * shape[dim + 1], *shape[dim + 2 :])


def gather_directly(shard, axis, dim):
    tiles = sent_to_all(shard, axis)
    return joined_along(tiles, dim)


def cut_along(shard, dim, devices):
    shape = shard.shape
    tiles = shard.reshape(*shape[:dim], devices, shape[dim] // devices, *shape[dim + 1 :])
    return jnp.moveaxis(tiles, dim, 0)


def sum_at_owner(shard, axis, dim):
    tiles = cut_along(shard, dim, lax.axis_size(axis))
    arrived = lax.all_to_all(tiles, axis, split_axis=0, concat_axis=0, tiled=True)
    return arrived.astype(jnp.float32).sum(axis=0)


def by_axis(shard, axes):
    for axis in axes:
        shard = lax.psum(shard, axis)
    return shard


def tile_products(source_rows, live_tiles, dest_slots, source_slots, row_tiles):
    source_tiles = source_rows.reshape(-1, 128, source_rows.shape[1])
    blocks = source_tiles[source_slots]
    products = jnp.einsum("src,sck->srk", live_tiles, blocks, preferred_element_type=jnp.float32)
    partial_value = jnp.zeros((row_tiles, 128, source_rows.shape[1]), jnp.float32)
    partial_value = partial_value.at[dest_slots].add(products)
    return partial_value.reshape(row_tiles * 128, source_rows.shape[1])


def local(tile_weights, tile_pos, tile_total, root_ids):
    col_devices = lax.axis_size(COL)
    row_index = lax.axis_index(ROW)
    col_index = lax.axis_index(COL)
    tile_data = tile_weights[0, 0]
    positions = tile_pos[0, 0]
    slot_limit = tile_total[0, 0]
    slot_total = tile_data.shape[0]
    in_use = (jnp.arange(slot_total, dtype=jnp.int32) < slot_limit).astype(jnp.bfloat16)
    live_tiles = tile_data * in_use[:, None, None]
    dest_slots = positions[0]
    source_slots = positions[1]
    row_block = col_devices * PV
    row_tiles = row_block // 128
    state_start = (row_index * col_devices + col_index) * PV
    state_rows = PV
    vertex_ids = state_start + jnp.arange(state_rows, dtype=jnp.int32)
    is_root = vertex_ids[:, None] == root_ids[None, :]
    kept_weight = is_root.astype(jnp.float32)
    path_now = is_root.astype(jnp.bfloat16)
    hop_level = jnp.where(is_root, 0, LEVELS + 1).astype(jnp.int32)
    found_counts = []
    found_totals = []
    for level_num in range(LEVELS):
        own_front = path_now
        source_rows = gather_directly(own_front, ROW, 0)
        partial_value = tile_products(source_rows, live_tiles, dest_slots, source_slots, row_tiles)
        arrived = sum_at_owner(partial_value.astype(jnp.bfloat16), COL, 0)
        newly = (arrived > 0) & (hop_level == LEVELS + 1)
        path_weight = jnp.where(newly, arrived, jnp.float32(0.0))
        hop_level = jnp.where(newly, jnp.int32(level_num + 1), hop_level)
        kept_weight = kept_weight + path_weight
        path_now = path_weight.astype(jnp.bfloat16)
        found_count = jnp.sum(newly.astype(jnp.float32), axis=0)
        found_total = jnp.sum(path_weight, axis=0)
        found_counts.append(found_count)
        found_totals.append(found_total)
    counts = jnp.stack(found_counts)
    totals = jnp.stack(found_totals)
    counts, totals = (by_axis(counts, ROW_COL), by_axis(totals, ROW_COL))
    factor = counts / jnp.maximum(totals, 1.0)
    factor_table = jnp.concatenate(
        [jnp.ones((1, ROOTS), jnp.float32), factor, jnp.zeros((1, ROOTS), jnp.float32)], axis=0
    )
    scale = jnp.zeros_like(kept_weight)
    for level_num in range(LEVELS + 2):
        scale = scale + jnp.where(
            hop_level == level_num, factor_table[level_num][None, :], jnp.float32(0.0)
        )
    return (hop_level, kept_weight * scale, counts)


def solution(mesh):
    torus = Mesh(mesh.devices.reshape(4, 4, 16, 2), ("row_0", "row_1", "col_0", "col_1"))
    return jax.shard_map(
        local,
        mesh=torus,
        in_specs=(P(ROW, COL, None, None, None), P(ROW, COL, None, None), P(ROW, COL), P()),
        out_specs=(P(ROW_COL, None), P(ROW_COL, None), P()),
        check_vma=False,
    )
```

profile of v0, /device:TPU:1, one launch (start us, length us, event | category | flops | bytes accessed | tf_op | source)
XLA Modules:
  0.0 243.6 jit_solution(7852062708470720910)
XLA Ops:
  0.7 0.8 compare_convert_fusion.1
  1.5 0.7 broadcast_in_dim.109
  2.1 7.6 %all-to-all-start = ((bf16[16,32,128]{2,1,0:T(8,128)(2,1)}), bf16[16,32,128]{2,1,0:T(8,128)(2,1)S(1)}, u32[]{:S(2)}, u32[]{:S(2)}) async-start(bf16[16,32,128]{2,1,0:T(8,128)(2,1)} %broadcast_in_dim.109), calls=%async_computation | async-start | bytes 262144 | tf_op jit(solution)/shard_map/all_to_all | solution.py:17
  9.7 0.8 fusion.24
  11.2 5.4 %all-to-all-done = bf16[16,32,128]{2,1,0:T(8,128)(2,1)S(1)} async-done(((bf16[16,32,128]{2,1,0:T(8,128)(2,1)}), bf16[16,32,128]{2,1,0:T(8,128)(2,1)S(1)}, u32[]{:S(2)}, u32[]{:S(2)}) %all-to-all-start) | async-done | bytes 131104 | tf_op jit(solution)/shard_map/all_to_all | solution.py:17
  16.6 0.7 gather_fusion
  17.3 1.8 fusion.3
  19.2 4.7 %scatter_fusion = f32[8,128,128]{2,1,0:T(8,128)S(1)} fusion(f32[8,128,128]{2,1,0:T(8,128)S(1)} %broadcast.213.clone.2, s32[32]{0:T(128)S(1)} %get-tuple-element.30, f32[32,128,128]{2,1,0:T(8,128)} %fusion.3), kind=kCustom, calls=%fused_computation.4 | custom fusion | flops 524288 | bytes 6291584 | tf_op jit(solution)/shard_map/scatter-add | solution.py:56
  23.9 39.1 %all_to_all.40 = bf16[32,32,128]{2,1,0:T(8,128)(2,1)S(1)} all-to-all(bf16[32,32,128]{2,1,0:T(8,128)(2,1)S(1)} %bitcast.48), channel_id=1, replica_groups=mesh['row_0'=4,'row_1'=4,'col_0'=16,'col_1'=2] {'col_0','col_1'}, dimensions={0} | all-to-all | bytes 524288 | tf_op jit(solution)/shard_map/all_to_all | solution.py:41
  63.3 9.6 %all_to_all.41 = bf16[16,32,128]{2,1,0:T(8,128)(2,1)S(1)} all-to-all(bf16[16,32,128]{2,1,0:T(8,128)(2,1)S(1)} %broadcast_in_dim.112), channel_id=1, replica_groups=mesh['row_0'=4,'row_1'=4,'col_0'=16,'col_1'=2] {'row_0','row_1'}, dimensions={0} | all-to-all | bytes 262144 | tf_op jit(solution)/shard_map/all_to_all | solution.py:17
  72.9 0.7 gather_fusion.1
  73.7 1.8 fusion.2
  75.5 4.7 %scatter_fusion.1 = f32[8,128,128]{2,1,0:T(8,128)S(1)} fusion(f32[8,128,128]{2,1,0:T(8,128)S(1)} %broadcast.213.clone.1, s32[32]{0:T(128)S(1)} %get-tuple-element.30, f32[32,128,128]{2,1,0:T(8,128)} %fusion.2), kind=kCustom, calls=%fused_computation.5 | custom fusion | flops 524288 | bytes 6291584 | tf_op jit(solution)/shard_map/scatter-add | solution.py:56
  80.3 27.1 %all_to_all.42 = bf16[32,32,128]{2,1,0:T(8,128)(2,1)S(1)} all-to-all(bf16[32,32,128]{2,1,0:T(8,128)(2,1)S(1)} %bitcast.49), channel_id=1, replica_groups=mesh['row_0'=4,'row_1'=4,'col_0'=16,'col_1'=2] {'col_0','col_1'}, dimensions={0} | all-to-all | bytes 524288 | tf_op jit(solution)/shard_map/all_to_all | solution.py:41
  107.4 0.1 select_reduce_fusion.2
  107.5 9.7 %all_to_all.43 = bf16[16,32,128]{2,1,0:T(8,128)(2,1)S(1)} all-to-all(bf16[16,32,128]{2,1,0:T(8,128)(2,1)S(1)} %broadcast_in_dim.114), channel_id=1, replica_groups=mesh['row_0'=4,'row_1'=4,'col_0'=16,'col_1'=2] {'row_0','row_1'}, dimensions={0} | all-to-all | bytes 262144 | tf_op jit(solution)/shard_map/all_to_all | solution.py:17
  117.2 0.7 gather_fusion.2
  117.9 1.8 fusion.1
  119.8 4.7 %scatter_fusion.2 = f32[8,128,128]{2,1,0:T(8,128)S(1)} fusion(f32[8,128,128]{2,1,0:T(8,128)S(1)} %broadcast.213.clone, s32[32]{0:T(128)S(1)} %get-tuple-element.30, f32[32,128,128]{2,1,0:T(8,128)} %fusion.1), kind=kCustom, calls=%fused_computation.6 | custom fusion | flops 524288 | bytes 6291584 | tf_op jit(solution)/shard_map/scatter-add | solution.py:56
  124.5 27.2 %all_to_all.44 = bf16[32,32,128]{2,1,0:T(8,128)(2,1)S(1)} all-to-all(bf16[32,32,128]{2,1,0:T(8,128)(2,1)S(1)} %bitcast.50), channel_id=1, replica_groups=mesh['row_0'=4,'row_1'=4,'col_0'=16,'col_1'=2] {'col_0','col_1'}, dimensions={0} | all-to-all | bytes 524288 | tf_op jit(solution)/shard_map/all_to_all | solution.py:41
  151.7 0.1 select_reduce_fusion.1
  151.9 9.7 %all_to_all.45 = bf16[16,32,128]{2,1,0:T(8,128)(2,1)S(1)} all-to-all(bf16[16,32,128]{2,1,0:T(8,128)(2,1)S(1)} %broadcast_in_dim.116), channel_id=1, replica_groups=mesh['row_0'=4,'row_1'=4,'col_0'=16,'col_1'=2] {'row_0','row_1'}, dimensions={0} | all-to-all | bytes 262144 | tf_op jit(solution)/shard_map/all_to_all | solution.py:17
  161.6 1.7 gather_fusion.3
  163.2 1.7 fusion
  165.0 2.7 %scatter_fusion.3 = f32[8,128,128]{2,1,0:T(8,128)S(1)} fusion(f32[8,128,128]{2,1,0:T(8,128)S(1)} %broadcast.213, s32[32]{0:T(128)S(1)} %get-tuple-element.30, f32[32,128,128]{2,1,0:T(8,128)S(1)} %fusion), kind=kCustom, calls=%fused_computation.7 | custom fusion | flops 524288 | bytes 6291584 | tf_op jit(solution)/shard_map/scatter-add | solution.py:56
  167.7 27.2 %all_to_all.46 = bf16[32,32,128]{2,1,0:T(8,128)(2,1)S(1)} all-to-all(bf16[32,32,128]{2,1,0:T(8,128)(2,1)S(1)} %bitcast.51), channel_id=1, replica_groups=mesh['row_0'=4,'row_1'=4,'col_0'=16,'col_1'=2] {'col_0','col_1'}, dimensions={0} | all-to-all | bytes 524288 | tf_op jit(solution)/shard_map/all_to_all | solution.py:41
  194.9 0.1 select_reduce_fusion
  195.0 6.9 %all-reduce.2 = (f32[4,128]{1,0:T(4,128)S(1)}, f32[4,128]{1,0:T(4,128)S(1)}) all-reduce(f32[4,128]{1,0:T(4,128)S(1)} %get-tuple-element.31, f32[4,128]{1,0:T(4,128)S(1)} %get-tuple-element.32), channel_id=1, replica_groups=mesh['row_0'=4,'row_1'=4,'col_0'=16,'col_1'=2] {'row_0'}, use_global_device_ids=true, to_apply=%region_12.13 | all-reduce | flops 1024 | bytes 8192 | tf_op jit(solution)/shard_map/psum | solution.py:47
  202.0 6.6 %all-reduce.1 = (f32[4,128]{1,0:T(4,128)S(1)}, f32[4,128]{1,0:T(4,128)S(1)}) all-reduce(f32[4,128]{1,0:T(4,128)S(1)} %get-tuple-element.15, f32[4,128]{1,0:T(4,128)S(1)} %get-tuple-element.16), channel_id=1, replica_groups=mesh['row_0'=4,'row_1'=4,'col_0'=16,'col_1'=2] {'row_1'}, use_global_device_ids=true, to_apply=%region_13.14 | all-reduce | flops 1024 | bytes 8192 | tf_op jit(solution)/shard_map/psum | solution.py:47
  208.6 20.3 %all-reduce = (f32[4,128]{1,0:T(4,128)S(1)}, f32[4,128]{1,0:T(4,128)S(1)}) all-reduce(f32[4,128]{1,0:T(4,128)S(1)} %get-tuple-element.13, f32[4,128]{1,0:T(4,128)S(1)} %get-tuple-element.14), channel_id=1, replica_groups=mesh['row_0'=4,'row_1'=4,'col_0'=16,'col_1'=2] {'col_0'}, use_global_device_ids=true, to_apply=%region_14.15 | all-reduce | flops 1024 | bytes 8192 | tf_op jit(solution)/shard_map/psum | solution.py:47
  228.9 14.0 %all-reduce.3 = (f32[4,128]{1,0:T(4,128)S(1)}, f32[4,128]{1,0:T(4,128)S(1)}) all-reduce(f32[4,128]{1,0:T(4,128)S(1)} %get-tuple-element.11, f32[4,128]{1,0:T(4,128)S(1)} %get-tuple-element.12), channel_id=1, replica_groups=mesh['row_0'=4,'row_1'=4,'col_0'=16,'col_1'=2] {'col_1'}, use_global_device_ids=true, to_apply=%region_15.16 | all-reduce | flops 1024 | bytes 8192 | tf_op jit(solution)/shard_map/psum | solution.py:47
  242.9 0.7 fusion.18
  (31 shorter events, 0.7 us)
Async XLA Ops:
  0.6 16.7 %copy-start = (bf16[1,1,32,128,128]{4,3,2,1,0:T(8,128)(2,1)S(1)}, bf16[1,1,32,128,128]{4,3,2,1,0:T(8,128)(2,1)}, u32[]{:S(2)}) copy-start(bf16[1,1,32,128,128]{4,3,2,1,0:T(8,128)(2,1)} %param.4) | copy-start | bytes 3145732
  2.1 14.4 %all-to-all-start = ((bf16[16,32,128]{2,1,0:T(8,128)(2,1)}), bf16[16,32,128]{2,1,0:T(8,128)(2,1)S(1)}, u32[]{:S(2)}, u32[]{:S(2)}) async-start(bf16[16,32,128]{2,1,0:T(8,128)(2,1)} %broadcast_in_dim.109), calls=%async_computation | async-start | bytes 262144 | tf_op jit(solution)/shard_map/all_to_all | solution.py:17
  19.2 43.9 %copy-start.1 = (s32[128]{0:T(128)S(1)}, s32[128]{0:T(128)}, u32[]{:S(2)}) copy-start(s32[128]{0:T(128)} %param.7) | copy-start | bytes 1540
  242.8 0.7 copy-start.2
where the time goes:
time: 244 us
  blocking collectives  197 us (81%)
  other arithmetic  19.7 us (8%)
  starting transfers between devices  7.58 us (3%)
  matrix products  7.22 us (3%)
  waiting for transfers between devices  5.4 us (2%)
  local copies, waits for them, and re-layouts  4.79 us (2%)
    all_to_all x4, blocking collectives, sum_at_owner(): lax.all_to_all(tiles, axis, split_axis=0, concat_axis=0, tiled=True)  121 us
    psum x4, blocking collectives, by_axis(): shard = lax.psum(shard, axis)  47.8 us
    all_to_all x3, blocking collectives, sent_to_all(): lax.all_to_all(jnp.broadcast_to(shard[None], (devices, *shard.shape)), ax...  29 us
    scatter-add x4, other arithmetic, tile_products(): partial_value = partial_value.at[dest_slots].add(products)  16.7 us
    all_to_all x1, starting transfers between devices, sent_to_all(): lax.all_to_all(jnp.broadcast_to(shard[None], (devices, *shard.shape)), ax...  7.58 us
    dot_general x4, matrix products, tile_products(): jnp.einsum('src,sck->srk', live_tiles, blocks, preferred_element_type=jnp...  7.22 us
    all_to_all x1, waiting for transfers between devices, sent_to_all(): lax.all_to_all(jnp.broadcast_to(shard[None], (devices, *shard.shape)), ax...  5.4 us
  transfers between devices with their start and end apart: 1, of which 1 were waited for; matrix products, arithmetic and copies ran while one was open for 0% of the time, Pallas kernels for 0%

commit v1 on v0

v1 whole, which is shorter than its diff:
```python
import jax
import jax.numpy as jnp
from jax import lax
from jax.experimental import pallas as pl
from jax.experimental.pallas import tpu as pltpu
from jax.sharding import Mesh
from jax.sharding import PartitionSpec as P

ROOTS = 128
HALF = ROOTS // 2
PV = 32
LEVELS = 4
TILE = 128
Y, X, Z, C = "y", "x", "z", "c"
ROW = (Y, X)
COL = (Z, C)
VMEM = pl.BlockSpec(memory_space=pltpu.VMEM)
SMEM = pl.BlockSpec(memory_space=pltpu.SMEM)
BF = jnp.bfloat16
F32 = jnp.float32


def build_kernel(pos_ref, total_ref, core_ref, tiles_ref, dense_ref):
    columns = dense_ref.shape[1] // 2
    core = core_ref[0]
    dense_ref[...] = jnp.zeros_like(dense_ref)

    def place(slot, carry):
        dest, source = pos_ref[0, slot], pos_ref[1, slot]
        for part in range(2):
            for half in range(2):
                first = pl.multiple_of(part * 2 * PV + (half ^ core) * PV, PV)
                rows = pl.multiple_of(dest * 2 * PV + part * PV, PV)
                lanes = pl.multiple_of(half * columns + source * TILE, TILE)
                dense_ref[pl.ds(rows, PV), pl.ds(lanes, TILE)] = tiles_ref[slot, pl.ds(first, PV), :]
        return carry

    lax.fori_loop(0, total_ref[0], place, 0)


def products(own_ref, other_ref, front, turned, sent_ref):
    rows = front.shape[0]
    left = lax.broadcasted_iota(jnp.int32, front.shape, 1) < HALF
    zero = jnp.zeros_like(front)

    def times(ref, half, value):
        return jnp.dot(
            ref[:, half * rows : (half + 1) * rows], value.astype(BF), preferred_element_type=F32
        )

    total = times(own_ref, 0, jnp.where(left, front, zero))
    total += times(own_ref, 1, jnp.where(left, zero, turned))
    total += times(other_ref, 0, jnp.where(left, zero, front))
    total += times(other_ref, 1, jnp.where(left, turned, zero))
    sent_ref[...] = total.astype(BF)


def first_kernel(base_ref, roots_ref, own_ref, other_ref, sent_ref):
    shape = sent_ref.shape
    row = lax.broadcasted_iota(jnp.int32, shape, 0)
    left = lax.broadcasted_iota(jnp.int32, shape, 1) < HALF
    vertex = (row // PV) * base_ref[2] + row % PV
    roots = roots_ref[...]
    front = (vertex + jnp.where(left, base_ref[0], base_ref[1]) == roots).astype(F32)
    turned = (vertex + jnp.where(left, base_ref[1], base_ref[0]) == roots).astype(F32)
    products(own_ref, other_ref, front, turned, sent_ref)


def level_kernel(front_ref, own_ref, other_ref, sent_ref):
    front = front_ref[...].astype(F32)
    products(own_ref, other_ref, front, pltpu.roll(front, HALF, 1), sent_ref)


def to_peers(value, axis):
    peers = lax.axis_size(axis)
    return lax.all_to_all(jnp.broadcast_to(value[None], (peers, *value.shape)), axis, 0, 0, tiled=True)


def local(tile_weights, tile_pos, tile_total, root_ids):
    rows_all, z_all = lax.axis_size(ROW), lax.axis_size(Z)
    row_index, z_index, core = lax.axis_index(ROW), lax.axis_index(Z), lax.axis_index(C)
    row_block = z_all * 2 * PV
    sources = rows_all * PV
    dests = z_all * PV
    own = pl.pallas_call(
        build_kernel,
        out_shape=jax.ShapeDtypeStruct((dests, 2 * sources), BF),
        in_specs=[SMEM, SMEM, SMEM, VMEM],
        out_specs=VMEM,
    )(tile_pos[0, 0], tile_total[0], core[None].astype(jnp.int32), tile_weights[0, 0])
    other = lax.ppermute(own, C, [(0, 1), (1, 0)])

    my_roots = lax.dynamic_slice_in_dim(root_ids, core * HALF, HALF)
    my_roots = jnp.concatenate([my_roots, my_roots])[None]
    base_own = z_index * 2 * PV + core * PV
    base_other = z_index * 2 * PV + (1 - core) * PV
    bases = jnp.stack([base_own, base_other, jnp.int32(row_block)]).astype(jnp.int32)
    offset = jnp.where(jnp.arange(ROOTS) < HALF, base_own, base_other)[None]
    vertex = row_index * row_block + jnp.arange(PV, dtype=jnp.int32)[:, None] + offset
    is_root = vertex == my_roots
    kept = is_root.astype(F32)
    hop = jnp.where(is_root, 0, LEVELS + 1).astype(jnp.int32)

    product_shape = jax.ShapeDtypeStruct((dests, ROOTS), BF)
    counts, totals = [], []
    front = None
    for level in range(1, LEVELS + 1):
        if level == 1:
            sent = pl.pallas_call(
                first_kernel, out_shape=product_shape, in_specs=[SMEM, VMEM, VMEM, VMEM], out_specs=VMEM
            )(bases, my_roots, own, other)
        else:
            front = to_peers(front, ROW).reshape(sources, ROOTS)
            sent = pl.pallas_call(
                level_kernel, out_shape=product_shape, in_specs=[VMEM] * 3, out_specs=VMEM
            )(front, own, other)
        arrived = lax.all_to_all(sent.reshape(z_all, PV, ROOTS), Z, 0, 0, tiled=True)
        arrived = arrived.astype(F32).sum(axis=0)
        newly = (arrived > 0) & (hop == LEVELS + 1)
        path = jnp.where(newly, arrived, 0.0)
        hop = jnp.where(newly, level, hop)
        kept = kept + path
        front = path.astype(BF)
        counts.append(newly.astype(F32).sum(axis=0))
        totals.append(path.sum(axis=0))

    theirs = jnp.concatenate([hop[:, HALF:].astype(F32), kept[:, HALF:]], axis=1)
    theirs = lax.ppermute(theirs, C, [(0, 1), (1, 0)])

    counts, totals = jnp.stack(counts), jnp.stack(totals)
    sums = jnp.concatenate(
        [counts[:, :HALF] + counts[:, HALF:], totals[:, :HALF] + totals[:, HALF:]], axis=1
    )
    sums = to_peers(sums, (Y, X, C)).reshape(rows_all, 2 * LEVELS, ROOTS).sum(axis=0)
    sums = to_peers(sums, Z).sum(axis=0).reshape(2, LEVELS, ROOTS)
    counts = jnp.concatenate([sums[0, :, :HALF], sums[1, :, :HALF]], axis=1)
    totals = jnp.concatenate([sums[0, :, HALF:], sums[1, :, HALF:]], axis=1)

    def joined(mine, received):
        return jnp.where(
            core == 0,
            jnp.concatenate([mine, received], axis=1),
            jnp.concatenate([received, mine], axis=1),
        )

    hop = joined(hop[:, :HALF], theirs[:, :HALF].astype(jnp.int32))
    kept = joined(kept[:, :HALF], theirs[:, HALF:])
    factor = counts / jnp.maximum(totals, 1.0)
    scale = jnp.where(hop == 0, 1.0, 0.0)
    for level in range(1, LEVELS + 1):
        scale = scale + jnp.where(hop == level, factor[level - 1][None], 0.0)
    return hop, kept * scale, counts


def solution(mesh):
    torus = Mesh(mesh.devices.reshape(4, 4, 16, 2), (Y, X, Z, C))
    return jax.shard_map(
        local,
        mesh=torus,
        in_specs=(P(ROW, COL, None, None, None), P(ROW, COL, None, None), P(ROW, COL), P()),
        out_specs=(P((Y, X, Z, C), None), P((Y, X, Z, C), None), P()),
        check_vma=False,
    )
```

time: 244 us -> 173 us (0.71)
  blocking collectives: 197 us -> 85.5 us
  starting transfers between devices: 7.58 us -> 35.4 us
  waiting for transfers between devices: 5.4 us -> 28.7 us
  other arithmetic: 19.7 us -> 3.75 us
  Pallas kernels: 0 us -> 14.3 us
  matrix products: 7.22 us -> 0 us
    all_to_all x7 -> x6, blocking collectives: 150 us -> 85.5 us  [the longest x3 51.5 us: local(): lax.all_to_all(sent.reshape(z_all, PV, ROOTS), Z, 0, 0, tiled=True)]
    psum x4 -> x0, blocking collectives: 47.8 us -> none  [by_axis(): shard = lax.psum(shard, axis)]
    all_to_all x1 -> x3, waiting for transfers between devices: 5.4 us -> 27.5 us  [the longest x2 15.4 us: to_peers(): lax.all_to_all(jnp.broadcast_to(value[None], (peers, *value.shape)), axis...]
    scatter-add x4 -> x0, other arithmetic: 16.7 us -> none  [tile_products(): partial_value = partial_value.at[dest_slots].add(products)]
    all_to_all x1 -> x3, starting transfers between devices: 7.58 us -> 24.1 us  [the longest x2 14.5 us: to_peers(): lax.all_to_all(jnp.broadcast_to(value[None], (peers, *value.shape)), axis...]
    pallas_call x0 -> x5, Pallas kernels: none -> 14.3 us  [the longest x3 8.97 us: local(): pl.pallas_call(level_kernel, out_shape=product_shape, in_specs=[VMEM] * 3...]
    ppermute x0 -> x2, starting transfers between devices: none -> 11.3 us  [the longest x1 8.72 us: local(): other = lax.ppermute(own, C, [(0, 1), (1, 0)])]
    dot_general x4 -> x0, matrix products: 7.22 us -> none  [tile_products(): jnp.einsum('src,sck->srk', live_tiles, blocks, preferred_element_type=jnp...]
  transfers between devices with their start and end apart: 1 -> 5, of which waited for: 1 -> 5; matrix products, arithmetic and copies ran while one was open for 0% -> 1% of each run, Pallas kernels for 0% -> 0%
where the time goes in v1:
time: 173 us; the launch traced here: 172 us
  blocking collectives  85.5 us (49%)
  starting transfers between devices  35.4 us (20%)
  waiting for transfers between devices  28.7 us (17%)
  Pallas kernels  14.3 us (8%)
  other arithmetic  3.75 us (2%)
  local copies, waits for them, and re-layouts  3.23 us (2%)
    all_to_all x3, blocking collectives, local(): lax.all_to_all(sent.reshape(z_all, PV, ROOTS), Z, 0, 0, tiled=True)  51.5 us
    all_to_all x3, blocking collectives, to_peers(): lax.all_to_all(jnp.broadcast_to(value[None], (peers, *value.shape)), axis...  34 us
    all_to_all x2, waiting for transfers between devices, to_peers(): lax.all_to_all(jnp.broadcast_to(value[None], (peers, *value.shape)), axis...  15.4 us
    all_to_all x2, starting transfers between devices, to_peers(): lax.all_to_all(jnp.broadcast_to(value[None], (peers, *value.shape)), axis...  14.5 us
    all_to_all x1, waiting for transfers between devices, local(): lax.all_to_all(sent.reshape(z_all, PV, ROOTS), Z, 0, 0, tiled=True)  12.1 us
    all_to_all x1, starting transfers between devices, local(): lax.all_to_all(sent.reshape(z_all, PV, ROOTS), Z, 0, 0, tiled=True)  9.58 us
    pallas_call x3, Pallas kernels, local(): pl.pallas_call(level_kernel, out_shape=product_shape, in_specs=[VMEM] * 3...  8.97 us
    ppermute x1, starting transfers between devices, local(): other = lax.ppermute(own, C, [(0, 1), (1, 0)])  8.72 us
  transfers between devices with their start and end apart: 5, of which 5 were waited for; matrix products, arithmetic and copies ran while one was open for 1% of the time, Pallas kernels for 0%

profile of v1, /device:TPU:1, one launch (start us, length us, event | category | flops | bytes accessed | tf_op | source)
XLA Modules:
  0.0 172.3 jit_solution(15830081523579172862)
XLA Ops:
  1.3 2.4 %shard_map.67.own_ref = bf16[512,1024]{1,0:T(8,128)(2,1)} custom-call(s32[2,32]{1,0:T(2,128)} %bitcast.62, s32[1]{0:T(128)} %bitcast.43.total_ref, s32[1]{0:T(128)} %bitcast.5.core_ref, bf16[32,128,128]{2,1,0:T(8,128)(2,1)} %bitcast.44), custom_call_target="tpu_custom_call" | custom-call | tf_op jit(solution)/shard_map/pallas_call | solution.py:85
  3.7 8.7 %collective-permute-start = (bf16[512,1024]{1,0:T(8,128)(2,1)}, bf16[512,1024]{1,0:T(8,128)(2,1)S(1)}, u32[]{:S(2)}, u32[]{:S(2)}) collective-permute-start(bf16[512,1024]{1,0:T(8,128)(2,1)} %shard_map.67.own_ref), channel_id=1, source_target_pairs={{0,1},{1,0},{2,3},{3,2},{4,5},{5,4},{6,7},{7,6},{8,9},{9,8},{10,11... | collective-permute-start | bytes 3145736 | tf_op jit(solution)/shard_map/ppermute | solution.py:91
  12.4 0.6 copy-done.1
  13.1 0.7 pad_add_fusion.1
  13.8 0.7 pad_add_fusion.base_ref
  14.4 0.4 collective-permute-done.other_ref
  14.9 1.0 copy-done
  15.9 2.9 %shard_map.68 = bf16[512,128]{1,0:T(8,128)(2,1)} custom-call(s32[3]{0:T(128)} %pad_add_fusion.base_ref, s32[1,128]{1,0:T(1,128)} %get-tuple-element.34.roots_ref, bf16[512,1024]{1,0:T(8,128)(2,1)} %shard_map.67.own_ref, bf16[512,1024]{1,0:T(8,128)(2,1)} %copy-done), custom_call_target="tpu_custom_call" | custom-call | tf_op jit(solution)/shard_map/pallas_call | solution.py:109
  18.8 9.6 %all-to-all-start = ((bf16[16,32,128]{2,1,0:T(8,128)(2,1)}), bf16[16,32,128]{2,1,0:T(8,128)(2,1)S(1)}, u32[]{:S(2)}, u32[]{:S(2)}) async-start(bf16[16,32,128]{2,1,0:T(8,128)(2,1)} %bitcast.45), calls=%async_computation | async-start | bytes 262144 | tf_op jit(solution)/shard_map/all_to_all | solution.py:117
  28.5 12.1 %all-to-all-done = bf16[16,32,128]{2,1,0:T(8,128)(2,1)S(1)} async-done(((bf16[16,32,128]{2,1,0:T(8,128)(2,1)}), bf16[16,32,128]{2,1,0:T(8,128)(2,1)S(1)}, u32[]{:S(2)}, u32[]{:S(2)}) %all-to-all-start) | async-done | bytes 131104 | tf_op jit(solution)/shard_map/all_to_all | solution.py:117
  40.7 13.8 %all_to_all.45 = bf16[16,32,128]{2,1,0:T(8,128)(2,1)} all-to-all(bf16[16,32,128]{2,1,0:T(8,128)(2,1)S(1)} %broadcast_in_dim.120), channel_id=1, replica_groups=mesh['y'=4,'x'=4,'z'=16,'c'=2] {'y','x'}, dimensions={0} | all-to-all | bytes 262144 | tf_op jit(solution)/shard_map/all_to_all | solution.py:76
  54.5 3.0 %shard_map.69 = bf16[512,128]{1,0:T(8,128)(2,1)} custom-call(bf16[512,128]{1,0:T(8,128)(2,1)} %bitcast.48, bf16[512,1024]{1,0:T(8,128)(2,1)} %shard_map.67.own_ref, bf16[512,1024]{1,0:T(8,128)(2,1)} %copy-done), custom_call_target="tpu_custom_call" | custom-call | tf_op jit(solution)/shard_map/pallas_call | solution.py:114
  57.5 18.4 %all_to_all.46 = bf16[16,32,128]{2,1,0:T(8,128)(2,1)S(1)} all-to-all(bf16[16,32,128]{2,1,0:T(8,128)(2,1)} %bitcast.49), channel_id=1, replica_groups=mesh['y'=4,'x'=4,'z'=16,'c'=2] {'z'}, dimensions={0} | all-to-all | bytes 262144 | tf_op jit(solution)/shard_map/all_to_all | solution.py:117
  76.0 0.1 convert_reduce_fusion.6
  76.1 10.1 %all_to_all.47 = bf16[16,32,128]{2,1,0:T(8,128)(2,1)} all-to-all(bf16[16,32,128]{2,1,0:T(8,128)(2,1)S(1)} %broadcast_in_dim.122), channel_id=1, replica_groups=mesh['y'=4,'x'=4,'z'=16,'c'=2] {'y','x'}, dimensions={0} | all-to-all | bytes 262144 | tf_op jit(solution)/shard_map/all_to_all | solution.py:76
  86.2 3.0 %shard_map.70 = bf16[512,128]{1,0:T(8,128)(2,1)} custom-call(bf16[512,128]{1,0:T(8,128)(2,1)} %bitcast.50, bf16[512,1024]{1,0:T(8,128)(2,1)} %shard_map.67.own_ref, bf16[512,1024]{1,0:T(8,128)(2,1)} %copy-done), custom_call_target="tpu_custom_call" | custom-call | tf_op jit(solution)/shard_map/pallas_call | solution.py:114
  89.2 17.0 %all_to_all.48 = bf16[16,32,128]{2,1,0:T(8,128)(2,1)S(1)} all-to-all(bf16[16,32,128]{2,1,0:T(8,128)(2,1)} %bitcast.51), channel_id=1, replica_groups=mesh['y'=4,'x'=4,'z'=16,'c'=2] {'z'}, dimensions={0} | all-to-all | bytes 262144 | tf_op jit(solution)/shard_map/all_to_all | solution.py:117
  106.2 0.1 convert_reduce_fusion.5
  106.4 10.1 %all_to_all.49 = bf16[16,32,128]{2,1,0:T(8,128)(2,1)} all-to-all(bf16[16,32,128]{2,1,0:T(8,128)(2,1)S(1)} %broadcast_in_dim.124), channel_id=1, replica_groups=mesh['y'=4,'x'=4,'z'=16,'c'=2] {'y','x'}, dimensions={0} | all-to-all | bytes 262144 | tf_op jit(solution)/shard_map/all_to_all | solution.py:76
  116.5 3.0 %shard_map.71 = bf16[512,128]{1,0:T(8,128)(2,1)} custom-call(bf16[512,128]{1,0:T(8,128)(2,1)} %bitcast.46, bf16[512,1024]{1,0:T(8,128)(2,1)} %shard_map.67.own_ref, bf16[512,1024]{1,0:T(8,128)(2,1)} %copy-done), custom_call_target="tpu_custom_call" | custom-call | tf_op jit(solution)/shard_map/pallas_call | solution.py:114
  119.5 16.0 %all_to_all.50 = bf16[16,32,128]{2,1,0:T(8,128)(2,1)S(1)} all-to-all(bf16[16,32,128]{2,1,0:T(8,128)(2,1)} %bitcast.47), channel_id=1, replica_groups=mesh['y'=4,'x'=4,'z'=16,'c'=2] {'z'}, dimensions={0} | all-to-all | bytes 262144 | tf_op jit(solution)/shard_map/all_to_all | solution.py:117
  135.5 0.1 convert_reduce_fusion.4
  136.0 0.6 broadcast_in_dim.128
  136.6 10.7 %all-to-all-start.7 = ((f32[32,4,128]{2,1,0:T(4,128)}), f32[32,4,128]{2,1,0:T(4,128)S(1)}, u32[]{:S(2)}, u32[]{:S(2)}) async-start(f32[32,4,128]{2,1,0:T(4,128)} %broadcast_in_dim.128), calls=%async_computation.7 | async-start | bytes 131072 | tf_op jit(solution)/shard_map/all_to_all | solution.py:76
  147.4 7.4 %all-to-all-done.7 = f32[32,4,128]{2,1,0:T(4,128)S(1)} async-done(((f32[32,4,128]{2,1,0:T(4,128)}), f32[32,4,128]{2,1,0:T(4,128)S(1)}, u32[]{:S(2)}, u32[]{:S(2)}) %all-to-all-start.7) | async-done | bytes 65568 | tf_op jit(solution)/shard_map/all_to_all | solution.py:76
  154.8 0.6 broadcast_in_dim.129
  155.4 3.8 %all-to-all-start.8 = ((f32[16,8,128]{2,1,0:T(8,128)}), f32[16,8,128]{2,1,0:T(8,128)S(1)}, u32[]{:S(2)}, u32[]{:S(2)}) async-start(f32[16,8,128]{2,1,0:T(8,128)} %broadcast_in_dim.129), calls=%async_computation.8 | async-start | bytes 131072 | tf_op jit(solution)/shard_map/all_to_all | solution.py:76
  159.3 2.6 %collective-permute-start.1 = (f32[32,128]{1,0:T(8,128)S(1)}, f32[32,128]{1,0:T(8,128)S(1)}, u32[]{:S(2)}, u32[]{:S(2)}) collective-permute-start(f32[32,128]{1,0:T(8,128)S(1)} %pad_maximum_fusion), channel_id=1, source_target_pairs={{0,1},{1,0},{2,3},{3,2},{4,5},{5,4},{6,7},{7,6},{8,9},{9,8},{10,11... | collective-permute-start | bytes 49160 | tf_op jit(solution)/shard_map/ppermute | solution.py:128
  161.9 0.8 collective-permute-done.1
  162.8 8.0 %all-to-all-done.8 = f32[16,8,128]{2,1,0:T(8,128)S(1)} async-done(((f32[16,8,128]{2,1,0:T(8,128)}), f32[16,8,128]{2,1,0:T(8,128)S(1)}, u32[]{:S(2)}, u32[]{:S(2)}) %all-to-all-start.8) | async-done | bytes 65568 | tf_op jit(solution)/shard_map/all_to_all | solution.py:76
  170.9 0.7 fusion.7
  171.6 0.7 fusion.2
  (30 shorter events, 1.1 us)
Async XLA Ops:
  3.7 11.2 %collective-permute-start = (bf16[512,1024]{1,0:T(8,128)(2,1)}, bf16[512,1024]{1,0:T(8,128)(2,1)S(1)}, u32[]{:S(2)}, u32[]{:S(2)}) collective-permute-start(bf16[512,1024]{1,0:T(8,128)(2,1)} %shard_map.67.own_ref), channel_id=1, source_target_pairs={{0,1},{1,0},{2,3},{3,2},{4,5},{5,4},{6,7},{7,6},{8,9},{9,8},{10,11... | collective-permute-start | bytes 3145736 | tf_op jit(solution)/shard_map/ppermute | solution.py:91
  12.4 0.7 copy-start.1
  14.9 1.0 copy-start
  18.8 21.7 %all-to-all-start = ((bf16[16,32,128]{2,1,0:T(8,128)(2,1)}), bf16[16,32,128]{2,1,0:T(8,128)(2,1)S(1)}, u32[]{:S(2)}, u32[]{:S(2)}) async-start(bf16[16,32,128]{2,1,0:T(8,128)(2,1)} %bitcast.45), calls=%async_computation | async-start | bytes 262144 | tf_op jit(solution)/shard_map/all_to_all | solution.py:117
  136.6 18.2 %all-to-all-start.7 = ((f32[32,4,128]{2,1,0:T(4,128)}), f32[32,4,128]{2,1,0:T(4,128)S(1)}, u32[]{:S(2)}, u32[]{:S(2)}) async-start(f32[32,4,128]{2,1,0:T(4,128)} %broadcast_in_dim.128), calls=%async_computation.7 | async-start | bytes 131072 | tf_op jit(solution)/shard_map/all_to_all | solution.py:76
  155.4 15.4 %all-to-all-start.8 = ((f32[16,8,128]{2,1,0:T(8,128)}), f32[16,8,128]{2,1,0:T(8,128)S(1)}, u32[]{:S(2)}, u32[]{:S(2)}) async-start(f32[16,8,128]{2,1,0:T(8,128)} %broadcast_in_dim.129), calls=%async_computation.8 | async-start | bytes 131072 | tf_op jit(solution)/shard_map/all_to_all | solution.py:76
  159.3 3.4 %collective-permute-start.1 = (f32[32,128]{1,0:T(8,128)S(1)}, f32[32,128]{1,0:T(8,128)S(1)}, u32[]{:S(2)}, u32[]{:S(2)}) collective-permute-start(f32[32,128]{1,0:T(8,128)S(1)} %pad_maximum_fusion), channel_id=1, source_target_pairs={{0,1},{1,0},{2,3},{3,2},{4,5},{5,4},{6,7},{7,6},{8,9},{9,8},{10,11... | collective-permute-start | bytes 49160 | tf_op jit(solution)/shard_map/ppermute | solution.py:128

commit v2 on v1

v2 whole, which is shorter than its diff:
```python
import functools

import jax
import jax.numpy as jnp
from jax import lax
from jax.experimental import pallas as pl
from jax.experimental.pallas import tpu as pltpu
from jax.sharding import Mesh
from jax.sharding import PartitionSpec as P

ROOTS = 128
HALF = ROOTS // 2
PV = 32
LEVELS = 4
TILE = 128
GRANT = 8 << 20
Y, X, Z, C = "y", "x", "z", "c"
ROW = (Y, X)
COL = (Z, C)
VMEM = pl.BlockSpec(memory_space=pltpu.VMEM)
SMEM = pl.BlockSpec(memory_space=pltpu.SMEM)
BF = jnp.bfloat16
F32 = jnp.float32


def call(kernel, out_shape, in_specs, *operands):
    return pl.pallas_call(
        kernel,
        out_shape=out_shape,
        in_specs=in_specs,
        out_specs=jax.tree.map(lambda _: VMEM, out_shape),
        compiler_params=pltpu.CompilerParams(vmem_limit_bytes=GRANT),
    )(*operands)


def build_kernel(pos_ref, total_ref, tiles_ref, dense_ref):
    columns = dense_ref.shape[1] // 2
    core = lax.axis_index(C)
    dense_ref[...] = jnp.zeros_like(dense_ref)

    def place(slot, carry):
        dest, source = pos_ref[0, slot], pos_ref[1, slot]
        for part in range(2):
            for half in range(2):
                first = pl.multiple_of(part * 2 * PV + (half ^ core) * PV, PV)
                rows = pl.multiple_of(dest * 2 * PV + part * PV, PV)
                lanes = pl.multiple_of(half * columns + source * TILE, TILE)
                dense_ref[pl.ds(rows, PV), pl.ds(lanes, TILE)] = tiles_ref[slot, pl.ds(first, PV), :]
        return carry

    lax.fori_loop(0, total_ref[0, 0], place, 0)


def left_half(shape):
    return lax.broadcasted_iota(jnp.int32, shape, len(shape) - 1) < HALF


def own_roots(roots_ref):
    roots = roots_ref[...]
    turned = pltpu.roll(roots, HALF, 1)
    return jnp.where(left_half(roots.shape) == (lax.axis_index(C) == 0), roots, turned)


def products(own_ref, other_ref, front, turned, sent_ref):
    rows = front.shape[0]
    left = left_half(front.shape)
    zero = jnp.zeros_like(front)

    def times(ref, half, value):
        return jnp.dot(
            ref[:, half * rows : (half + 1) * rows], value.astype(BF), preferred_element_type=F32
        )

    total = times(own_ref, 0, jnp.where(left, front, zero))
    total += times(own_ref, 1, jnp.where(left, zero, turned))
    total += times(other_ref, 0, jnp.where(left, zero, front))
    total += times(other_ref, 1, jnp.where(left, turned, zero))
    sent_ref[...] = total.astype(BF)


def first_kernel(row_block, roots_ref, own_ref, other_ref, sent_ref, hop_ref, kept_ref):
    core, pair = lax.axis_index(C), lax.axis_index(Z) * 2 * PV
    base_own, base_other = pair + core * PV, pair + (1 - core) * PV
    roots = own_roots(roots_ref)
    shape = (own_ref.shape[1] // 2, ROOTS)
    row = lax.broadcasted_iota(jnp.int32, shape, 0)
    left = left_half(shape)
    vertex = (row // PV) * row_block + row % PV
    front = (vertex + jnp.where(left, base_own, base_other) == roots).astype(F32)
    turned = (vertex + jnp.where(left, base_other, base_own) == roots).astype(F32)
    products(own_ref, other_ref, front, turned, sent_ref)
    state = hop_ref.shape
    vertex = lax.broadcasted_iota(jnp.int32, state, 0) + lax.axis_index(ROW) * row_block
    is_root = vertex + jnp.where(left_half(state), base_own, base_other) == roots
    kept_ref[...] = is_root.astype(F32)
    hop_ref[...] = jnp.where(is_root, 0, LEVELS + 1)


def level_kernel(front_ref, own_ref, other_ref, sent_ref):
    front = front_ref[...].astype(F32)
    products(own_ref, other_ref, front, pltpu.roll(front, HALF, 1), sent_ref)


def found(level, parts_ref, hop_ref, kept_ref):
    arrived = parts_ref[0].astype(F32)
    for peer in range(1, parts_ref.shape[0]):
        arrived += parts_ref[peer].astype(F32)
    hop = hop_ref[...]
    newly = (arrived > 0) & (hop == LEVELS + 1)
    path = jnp.where(newly, arrived, 0.0)
    return jnp.where(newly, level, hop), kept_ref[...] + path, path


def update_kernel(level, parts_ref, hop_in, kept_in, hop_ref, kept_ref, front_ref):
    hop_ref[...], kept_ref[...], path = found(level, parts_ref, hop_in, kept_in)
    path = path.astype(BF)
    for peer in range(front_ref.shape[0]):
        front_ref[peer] = path


def last_kernel(parts_ref, hop_in, kept_in, mine_ref, theirs_ref, sums_ref):
    hop, kept, _ = found(LEVELS, parts_ref, hop_in, kept_in)
    hops = hop.astype(F32)
    left = left_half(hop.shape)
    mine_ref[...] = jnp.where(left, hops, pltpu.roll(kept, HALF, 1))
    theirs_ref[...] = jnp.where(left, pltpu.roll(hops, HALF, 1), kept)
    sums = []
    for level in range(1, LEVELS + 1):
        at = hop == level
        count = jnp.sum(at.astype(F32), axis=0, keepdims=True)
        total = jnp.sum(jnp.where(at, kept, 0.0), axis=0, keepdims=True)
        count, total = count + pltpu.roll(count, HALF, 1), total + pltpu.roll(total, HALF, 1)
        sums.append(jnp.where(left_half(count.shape), count, total))
    sums = jnp.concatenate(sums, axis=0)
    for peer in range(sums_ref.shape[0]):
        sums_ref[peer] = sums


def sum_kernel(parts_ref, sums_ref):
    sums = jnp.sum(parts_ref[...], axis=0)
    for peer in range(sums_ref.shape[0]):
        sums_ref[peer] = sums


def end_kernel(sums_ref, mine_ref, theirs_ref, hop_ref, share_ref, counts_ref):
    parts = sums_ref[...]
    sums = jnp.sum(parts.reshape(parts.shape[0] // 2, 2, *parts.shape[1:]), axis=0)
    first, second = sums[0], sums[1]
    left = left_half(first.shape)
    counts = jnp.where(left, first, pltpu.roll(second, HALF, 1))
    totals = jnp.where(left, pltpu.roll(first, HALF, 1), second)
    counts_ref[...] = counts
    factor = counts / jnp.maximum(totals, 1.0)
    mine, theirs = mine_ref[...], theirs_ref[...]
    is_first = lax.axis_index(C) == 0
    low, high = jnp.where(is_first, mine, theirs), jnp.where(is_first, theirs, mine)
    left = left_half(low.shape)
    hop = jnp.where(left, low, pltpu.roll(high, HALF, 1)).astype(jnp.int32)
    kept = jnp.where(left, pltpu.roll(low, HALF, 1), high)
    scale = jnp.where(hop == 0, 1.0, 0.0)
    for level in range(1, LEVELS + 1):
        scale = jnp.where(hop == level, factor[level - 1 : level], scale)
    hop_ref[...] = hop
    share_ref[...] = kept * scale


def exchanged(value, axis):
    return lax.all_to_all(value, axis, 0, 0, tiled=True)


def local(tile_weights, tile_pos, tile_total, root_ids):
    rows_all, z_all = lax.axis_size(ROW), lax.axis_size(Z)
    row_block, sources, dests = z_all * 2 * PV, rows_all * PV, z_all * PV
    bf = lambda *shape: jax.ShapeDtypeStruct(shape, BF)
    f32 = lambda *shape: jax.ShapeDtypeStruct(shape, F32)
    hops = jax.ShapeDtypeStruct((PV, ROOTS), jnp.int32)
    swap = [(0, 1), (1, 0)]

    own = call(build_kernel, bf(dests, 2 * sources), [SMEM, SMEM, VMEM], tile_pos[0, 0], tile_total, tile_weights[0, 0])
    other = lax.ppermute(own, C, swap)
    sent, hop, kept = call(
        functools.partial(first_kernel, row_block),
        (bf(dests, ROOTS), hops, f32(PV, ROOTS)),
        [VMEM] * 3,
        root_ids[None],
        own,
        other,
    )
    for level in range(1, LEVELS):
        parts = exchanged(sent.reshape(z_all, PV, ROOTS), Z)
        hop, kept, front = call(
            functools.partial(update_kernel, level),
            (hops, f32(PV, ROOTS), bf(rows_all, PV, ROOTS)),
            [VMEM] * 3,
            parts,
            hop,
            kept,
        )
        front = exchanged(front, ROW).reshape(sources, ROOTS)
        sent = call(level_kernel, bf(dests, ROOTS), [VMEM] * 3, front, own, other)
    parts = exchanged(sent.reshape(z_all, PV, ROOTS), Z)
    mine, theirs, sums = call(
        last_kernel,
        (f32(PV, ROOTS), f32(PV, ROOTS), f32(z_all, LEVELS, ROOTS)),
        [VMEM] * 3,
        parts,
        hop,
        kept,
    )
    theirs = lax.ppermute(theirs, C, swap)
    sums = exchanged(sums, Z)
    sums = call(sum_kernel, f32(2 * rows_all, LEVELS, ROOTS), [VMEM], sums)
    sums = exchanged(sums, (Y, X, C))
    return call(end_kernel, (hops, f32(PV, ROOTS), f32(LEVELS, ROOTS)), [VMEM] * 3, sums, mine, theirs)


def solution(mesh):
    torus = Mesh(mesh.devices.reshape(4, 4, 16, 2), (Y, X, Z, C))
    return jax.shard_map(
        local,
        mesh=torus,
        in_specs=(P(ROW, COL, None, None, None), P(ROW, COL, None, None), P(ROW, COL), P()),
        out_specs=(P((Y, X, Z, C), None), P((Y, X, Z, C), None), P()),
        check_vma=False,
    )
```

time: 173 us -> 161 us (0.931)
  blocking collectives: 85.5 us -> 121 us
  waiting for transfers between devices: 28.7 us -> 7.43 us
  starting transfers between devices: 35.4 us -> 22.5 us
  Pallas kernels: 14.3 us -> 5.73 us
  other arithmetic: 3.75 us -> 0 us
    all_to_all x6 -> x8, blocking collectives: 85.5 us -> 121 us  [exchanged(): return lax.all_to_all(value, axis, 0, 0, tiled=True)]
    all_to_all x3 -> x1, waiting for transfers between devices: 27.5 us -> 4.35 us  [exchanged(): return lax.all_to_all(value, axis, 0, 0, tiled=True)]
    all_to_all x3 -> x1, starting transfers between devices: 24.1 us -> 11.7 us  [exchanged(): return lax.all_to_all(value, axis, 0, 0, tiled=True)]
    pallas_call x5 -> x11, Pallas kernels: 14.3 us -> 5.73 us  [call(): pl.pallas_call(kernel, out_shape=out_shape, in_specs=in_specs, out_specs=...]
    ppermute x2, waiting for transfers between devices: 1.23 us -> 3.08 us  [the longest x1 2.26 us: local(): other = lax.ppermute(own, C, swap)]
  transfers between devices with their start and end apart: 5 -> 3, of which waited for: 5 -> 3; matrix products, arithmetic and copies ran while one was open for 1% -> 0% of each run, Pallas kernels for 0% -> 0%
where the time goes in v2:
time: 161 us; the launch traced here: 160 us
  blocking collectives  121 us (75%)
  starting transfers between devices  22.5 us (14%)
  waiting for transfers between devices  7.43 us (5%)
  Pallas kernels  5.73 us (4%)
  local copies, waits for them, and re-layouts  1.9 us (1%)
    all_to_all x8, blocking collectives, exchanged(): return lax.all_to_all(value, axis, 0, 0, tiled=True)  121 us
    all_to_all x1, starting transfers between devices, exchanged(): return lax.all_to_all(value, axis, 0, 0, tiled=True)  11.7 us
    ppermute x1, starting transfers between devices, local(): other = lax.ppermute(own, C, swap)  8.46 us
    pallas_call x11, Pallas kernels, call(): pl.pallas_call(kernel, out_shape=out_shape, in_specs=in_specs, out_specs=...  5.73 us
    all_to_all x1, waiting for transfers between devices, exchanged(): return lax.all_to_all(value, axis, 0, 0, tiled=True)  4.35 us
  transfers between devices with their start and end apart: 3, of which 3 were waited for; matrix products, arithmetic and copies ran while one was open for 0% of the time, Pallas kernels for 0%

profile of v2, /device:TPU:1, one launch (start us, length us, event | category | flops | bytes accessed | tf_op | source)
XLA Modules:
  0.0 160.1 jit_solution(9433613081117768944)
XLA Ops:
  1.3 0.0 copy-start.1
  1.3 0.7 copy-done.1
  2.0 0.0 copy-start
  2.0 1.2 copy-done
  3.2 1.1 shard_map.67.own_ref
  4.3 0.0 copy-start.2
  4.3 8.5 %collective-permute-start = (bf16[512,1024]{1,0:T(8,128)(2,1)S(1)}, bf16[512,1024]{1,0:T(8,128)(2,1)S(1)}, u32[]{:S(2)}, u32[]{:S(2)}) collective-permute-start(bf16[512,1024]{1,0:T(8,128)(2,1)S(1)} %shard_map.67.own_ref), channel_id=1, source_target_pairs={{0,1},{1,0},{2,3},{3,2},{4,5},{5,4},{6,7},{7,6},{8,9},{9,8},{10,11... | collective-permute-start | bytes 3145736 | tf_op jit(solution)/shard_map/ppermute | solution.py:180
  12.8 2.3 %collective-permute-done.other_ref = bf16[512,1024]{1,0:T(8,128)(2,1)S(1)} collective-permute-done((bf16[512,1024]{1,0:T(8,128)(2,1)S(1)}, bf16[512,1024]{1,0:T(8,128)(2,1)S(1)}, u32[]{:S(2)}, u32[]{:S(2)}) %collective-permute-start) | collective-permute-done | bytes 1048608 | tf_op jit(solution)/shard_map/ppermute | solution.py:180
  15.0 0.0 copy-done.2
  15.0 0.8 shard_map.68
  15.8 21.8 %all_to_all.45.parts_ref = bf16[16,32,128]{2,1,0:T(8,128)(2,1)S(1)} all-to-all(bf16[16,32,128]{2,1,0:T(8,128)(2,1)S(1)} %bitcast.17), channel_id=1, replica_groups=mesh['y'=4,'x'=4,'z'=16,'c'=2] {'z'}, dimensions={0} | all-to-all | bytes 262144 | tf_op jit(solution)/shard_map/all_to_all | solution.py:168
  37.7 13.2 %all_to_all.46 = bf16[16,32,128]{2,1,0:T(8,128)(2,1)S(1)} all-to-all(bf16[16,32,128]{2,1,0:T(8,128)(2,1)S(1)} %get-tuple-element.21), channel_id=1, replica_groups=mesh['y'=4,'x'=4,'z'=16,'c'=2] {'y','x'}, dimensions={0} | all-to-all | bytes 262144 | tf_op jit(solution)/shard_map/all_to_all | solution.py:168
  50.9 0.8 shard_map.70
  51.6 18.2 %all_to_all.47.parts_ref = bf16[16,32,128]{2,1,0:T(8,128)(2,1)S(1)} all-to-all(bf16[16,32,128]{2,1,0:T(8,128)(2,1)S(1)} %bitcast.14), channel_id=1, replica_groups=mesh['y'=4,'x'=4,'z'=16,'c'=2] {'z'}, dimensions={0} | all-to-all | bytes 262144 | tf_op jit(solution)/shard_map/all_to_all | solution.py:168
  69.9 9.9 %all_to_all.48 = bf16[16,32,128]{2,1,0:T(8,128)(2,1)S(1)} all-to-all(bf16[16,32,128]{2,1,0:T(8,128)(2,1)S(1)} %get-tuple-element.24), channel_id=1, replica_groups=mesh['y'=4,'x'=4,'z'=16,'c'=2] {'y','x'}, dimensions={0} | all-to-all | bytes 262144 | tf_op jit(solution)/shard_map/all_to_all | solution.py:168
  79.8 0.8 shard_map.72
  80.6 17.0 %all_to_all.49.parts_ref = bf16[16,32,128]{2,1,0:T(8,128)(2,1)S(1)} all-to-all(bf16[16,32,128]{2,1,0:T(8,128)(2,1)S(1)} %bitcast.16), channel_id=1, replica_groups=mesh['y'=4,'x'=4,'z'=16,'c'=2] {'z'}, dimensions={0} | all-to-all | bytes 262144 | tf_op jit(solution)/shard_map/all_to_all | solution.py:168
  97.6 9.9 %all_to_all.50 = bf16[16,32,128]{2,1,0:T(8,128)(2,1)S(1)} all-to-all(bf16[16,32,128]{2,1,0:T(8,128)(2,1)S(1)} %get-tuple-element.27), channel_id=1, replica_groups=mesh['y'=4,'x'=4,'z'=16,'c'=2] {'y','x'}, dimensions={0} | all-to-all | bytes 262144 | tf_op jit(solution)/shard_map/all_to_all | solution.py:168
  107.5 0.8 shard_map.74
  108.3 15.8 %all_to_all.51.parts_ref = bf16[16,32,128]{2,1,0:T(8,128)(2,1)S(1)} all-to-all(bf16[16,32,128]{2,1,0:T(8,128)(2,1)S(1)} %bitcast.12), channel_id=1, replica_groups=mesh['y'=4,'x'=4,'z'=16,'c'=2] {'z'}, dimensions={0} | all-to-all | bytes 262144 | tf_op jit(solution)/shard_map/all_to_all | solution.py:168
  124.1 0.1 shard_map.75
  124.2 15.3 %all_to_all.52.parts_ref = f32[16,4,128]{2,1,0:T(4,128)S(1)} all-to-all(f32[16,4,128]{2,1,0:T(4,128)S(1)} %get-tuple-element.30), channel_id=1, replica_groups=mesh['y'=4,'x'=4,'z'=16,'c'=2] {'z'}, dimensions={0} | all-to-all | bytes 65536 | tf_op jit(solution)/shard_map/all_to_all | solution.py:168
  139.6 0.6 shard_map.76
  140.2 11.7 %all-to-all-start.8 = ((f32[32,4,128]{2,1,0:T(4,128)}), f32[32,4,128]{2,1,0:T(4,128)S(1)}, u32[]{:S(2)}, u32[]{:S(2)}) async-start(f32[32,4,128]{2,1,0:T(4,128)} %shard_map.76), calls=%async_computation.8 | async-start | bytes 131072 | tf_op jit(solution)/shard_map/all_to_all | solution.py:168
  152.0 2.3 %collective-permute-start.1 = (f32[32,128]{1,0:T(8,128)S(1)}, f32[32,128]{1,0:T(8,128)S(1)}, u32[]{:S(2)}, u32[]{:S(2)}) collective-permute-start(f32[32,128]{1,0:T(8,128)S(1)} %get-tuple-element.32), channel_id=1, source_target_pairs={{0,1},{1,0},{2,3},{3,2},{4,5},{5,4},{6,7},{7,6},{8,9},{9,8},{10,11... | collective-permute-start | bytes 49160 | tf_op jit(solution)/shard_map/ppermute | solution.py:210
  154.2 0.8 collective-permute-done.1.theirs_ref
  155.0 4.4 %all-to-all-done.8.sums_ref = f32[32,4,128]{2,1,0:T(4,128)S(1)} async-done(((f32[32,4,128]{2,1,0:T(4,128)}), f32[32,4,128]{2,1,0:T(4,128)S(1)}, u32[]{:S(2)}, u32[]{:S(2)}) %all-to-all-start.8) | async-done | bytes 65568 | tf_op jit(solution)/shard_map/all_to_all | solution.py:168
  159.4 0.7 shard_map.77
  (3 shorter events, 0.1 us)
Async XLA Ops:
  1.3 0.7 copy-start.1
  2.0 1.2 copy-start
  4.3 10.7 %copy-start.2 = (s32[128]{0:T(128)S(1)}, s32[128]{0:T(128)}, u32[]{:S(2)}) copy-start(s32[128]{0:T(128)} %param.7) | copy-start | bytes 1540
  4.3 10.7 %collective-permute-start = (bf16[512,1024]{1,0:T(8,128)(2,1)S(1)}, bf16[512,1024]{1,0:T(8,128)(2,1)S(1)}, u32[]{:S(2)}, u32[]{:S(2)}) collective-permute-start(bf16[512,1024]{1,0:T(8,128)(2,1)S(1)} %shard_map.67.own_ref), channel_id=1, source_target_pairs={{0,1},{1,0},{2,3},{3,2},{4,5},{5,4},{6,7},{7,6},{8,9},{9,8},{10,11... | collective-permute-start | bytes 3145736 | tf_op jit(solution)/shard_map/ppermute | solution.py:180
  140.2 19.2 %all-to-all-start.8 = ((f32[32,4,128]{2,1,0:T(4,128)}), f32[32,4,128]{2,1,0:T(4,128)S(1)}, u32[]{:S(2)}, u32[]{:S(2)}) async-start(f32[32,4,128]{2,1,0:T(4,128)} %shard_map.76), calls=%async_computation.8 | async-start | bytes 131072 | tf_op jit(solution)/shard_map/all_to_all | solution.py:168
  152.0 3.1 %collective-permute-start.1 = (f32[32,128]{1,0:T(8,128)S(1)}, f32[32,128]{1,0:T(8,128)S(1)}, u32[]{:S(2)}, u32[]{:S(2)}) collective-permute-start(f32[32,128]{1,0:T(8,128)S(1)} %get-tuple-element.32), channel_id=1, source_target_pairs={{0,1},{1,0},{2,3},{3,2},{4,5},{5,4},{6,7},{7,6},{8,9},{9,8},{10,11... | collective-permute-start | bytes 49160 | tf_op jit(solution)/shard_map/ppermute | solution.py:210

commit v3 on v2

--- a/solution.py
+++ b/solution.py
@@ -14,28 +14,39 @@
 LEVELS = 4
 TILE = 128
 GRANT = 8 << 20
+BUILD_GRANT = 209 << 18
+CHUNKS = 4
 Y, X, Z, C = "y", "x", "z", "c"
 ROW = (Y, X)
 COL = (Z, C)
 VMEM = pl.BlockSpec(memory_space=pltpu.VMEM)
 SMEM = pl.BlockSpec(memory_space=pltpu.SMEM)
+ANY = pl.BlockSpec(memory_space=pl.ANY)
 BF = jnp.bfloat16
 F32 = jnp.float32
 
 
-def call(kernel, out_shape, in_specs, *operands):
+def call(kernel, out_shape, in_specs, *operands, scratch=(), grant=GRANT):
     return pl.pallas_call(
         kernel,
         out_shape=out_shape,
         in_specs=in_specs,
         out_specs=jax.tree.map(lambda _: VMEM, out_shape),
-        compiler_params=pltpu.CompilerParams(vmem_limit_bytes=GRANT),
+        scratch_shapes=scratch,
+        compiler_params=pltpu.CompilerParams(vmem_limit_bytes=grant),
     )(*operands)
 
 
-def build_kernel(pos_ref, total_ref, tiles_ref, dense_ref):
+def build_kernel(total_ref, pos_ref, tiles_any, dense_ref, tiles_ref, tile_sems):
     columns = dense_ref.shape[1] // 2
     core = lax.axis_index(C)
+    slots = tiles_ref.shape[0]
+    step = slots // CHUNKS
+    tile_copies = []
+    for chunk in range(CHUNKS):
+        part = pl.ds(chunk * step, step)
+        tile_copies.append(pltpu.make_async_copy(tiles_any.at[part], tiles_ref.at[part], tile_sems.at[chunk]))
+        tile_copies[-1].start()
     dense_ref[...] = jnp.zeros_like(dense_ref)
 
     def place(slot, carry):
@@ -48,7 +59,9 @@
                 dense_ref[pl.ds(rows, PV), pl.ds(lanes, TILE)] = tiles_ref[slot, pl.ds(first, PV), :]
         return carry
 
-    lax.fori_loop(0, total_ref[0, 0], place, 0)
+    for chunk in range(CHUNKS):
+        tile_copies[chunk].wait()
+        lax.fori_loop(chunk * step, jnp.minimum(total_ref[0, 0], (chunk + 1) * step), place, 0)
 
 
 def left_half(shape):
@@ -61,44 +74,58 @@
     return jnp.where(left_half(roots.shape) == (lax.axis_index(C) == 0), roots, turned)
 
 
-def products(own_ref, other_ref, front, turned, sent_ref):
-    rows = front.shape[0]
+def times(ref, half, value):
+    rows = value.shape[0]
+    return jnp.dot(ref[:, half * rows : (half + 1) * rows], value.astype(BF), preferred_element_type=F32)
+
+
+def own_products(own_ref, front, turned):
     left = left_half(front.shape)
     zero = jnp.zeros_like(front)
-
-    def times(ref, half, value):
-        return jnp.dot(
-            ref[:, half * rows : (half + 1) * rows], value.astype(BF), preferred_element_type=F32
-        )
-
-    total = times(own_ref, 0, jnp.where(left, front, zero))
-    total += times(own_ref, 1, jnp.where(left, zero, turned))
-    total += times(other_ref, 0, jnp.where(left, zero, front))
-    total += times(other_ref, 1, jnp.where(left, turned, zero))
-    sent_ref[...] = total.astype(BF)
-
-
-def first_kernel(row_block, roots_ref, own_ref, other_ref, sent_ref, hop_ref, kept_ref):
+    return times(own_ref, 0, jnp.where(left, front, zero)) + times(own_ref, 1, jnp.where(left, zero, turned))
+
+
+def other_products(other_ref, front, turned):
+    left = left_half(front.shape)
+    zero = jnp.zeros_like(front)
+    return times(other_ref, 0, jnp.where(left, zero, front)) + times(other_ref, 1, jnp.where(left, turned, zero))
+
+
+def root_front(row_block, roots_ref, sources):
     core, pair = lax.axis_index(C), lax.axis_index(Z) * 2 * PV
     base_own, base_other = pair + core * PV, pair + (1 - core) * PV
     roots = own_roots(roots_ref)
-    shape = (own_ref.shape[1] // 2, ROOTS)
+    shape = (sources, ROOTS)
     row = lax.broadcasted_iota(jnp.int32, shape, 0)
     left = left_half(shape)
     vertex = (row // PV) * row_block + row % PV
     front = (vertex + jnp.where(left, base_own, base_other) == roots).astype(F32)
     turned = (vertex + jnp.where(left, base_other, base_own) == roots).astype(F32)
-    products(own_ref, other_ref, front, turned, sent_ref)
+    return front, turned
+
+
+def first_own_kernel(row_block, roots_ref, own_ref, part_ref, hop_ref, kept_ref):
+    front, turned = root_front(row_block, roots_ref, own_ref.shape[1] // 2)
+    part_ref[...] = own_products(own_ref, front, turned)
+    core, pair = lax.axis_index(C), lax.axis_index(Z) * 2 * PV
+    base_own, base_other = pair + core * PV, pair + (1 - core) * PV
     state = hop_ref.shape
     vertex = lax.broadcasted_iota(jnp.int32, state, 0) + lax.axis_index(ROW) * row_block
-    is_root = vertex + jnp.where(left_half(state), base_own, base_other) == roots
+    is_root = vertex + jnp.where(left_half(state), base_own, base_other) == own_roots(roots_ref)
     kept_ref[...] = is_root.astype(F32)
     hop_ref[...] = jnp.where(is_root, 0, LEVELS + 1)
 
 
+def first_other_kernel(row_block, roots_ref, other_ref, part_ref, sent_ref):
+    front, turned = root_front(row_block, roots_ref, other_ref.shape[1] // 2)
+    sent_ref[...] = (part_ref[...] + other_products(other_ref, front, turned)).astype(BF)
+
+
 def level_kernel(front_ref, own_ref, other_ref, sent_ref):
     front = front_ref[...].astype(F32)
-    products(own_ref, other_ref, front, pltpu.roll(front, HALF, 1), sent_ref)
+    turned = pltpu.roll(front, HALF, 1)
+    total = own_products(own_ref, front, turned) + other_products(other_ref, front, turned)
+    sent_ref[...] = total.astype(BF)
 
 
 def found(level, parts_ref, hop_ref, kept_ref):
@@ -176,15 +203,35 @@
     hops = jax.ShapeDtypeStruct((PV, ROOTS), jnp.int32)
     swap = [(0, 1), (1, 0)]
 
-    own = call(build_kernel, bf(dests, 2 * sources), [SMEM, SMEM, VMEM], tile_pos[0, 0], tile_total, tile_weights[0, 0])
+    slots = tile_weights.shape[2]
+    own = call(
+        build_kernel,
+        bf(dests, 2 * sources),
+        [SMEM, SMEM, ANY],
+        tile_total,
+        tile_pos[0, 0],
+        tile_weights[0, 0],
+        grant=BUILD_GRANT,
+        scratch=[
+            pltpu.VMEM((slots, TILE, TILE), BF),
+            pltpu.SemaphoreType.DMA((CHUNKS,)),
+        ],
+    )
     other = lax.ppermute(own, C, swap)
-    sent, hop, kept = call(
-        functools.partial(first_kernel, row_block),
-        (bf(dests, ROOTS), hops, f32(PV, ROOTS)),
+    part, hop, kept = call(
+        functools.partial(first_own_kernel, row_block),
+        (f32(dests, ROOTS), hops, f32(PV, ROOTS)),
+        [VMEM] * 2,
+        root_ids[None],
+        own,
+    )
+    sent = call(
+        functools.partial(first_other_kernel, row_block),
+        bf(dests, ROOTS),
         [VMEM] * 3,
         root_ids[None],
-        own,
         other,
+        part,
     )
     for level in range(1, LEVELS):
         parts = exchanged(sent.reshape(z_all, PV, ROOTS), Z)

time: 161 us -> 160 us (level)
    pallas_call x11 -> x12, Pallas kernels: 5.73 us -> 6.67 us  [call(): pl.pallas_call(kernel, out_shape=out_shape, in_specs=in_specs, out_specs=...]
where the time goes in v3:
time: 160 us
  blocking collectives  121 us (76%)
  starting transfers between devices  23 us (14%)
  waiting for transfers between devices  6.91 us (4%)
  Pallas kernels  6.67 us (4%)
    all_to_all x8, blocking collectives, exchanged(): return lax.all_to_all(value, axis, 0, 0, tiled=True)  121 us
    all_to_all x1, starting transfers between devices, exchanged(): return lax.all_to_all(value, axis, 0, 0, tiled=True)  11.7 us
    ppermute x1, starting transfers between devices, local(): other = lax.ppermute(own, C, swap)  9.03 us
    pallas_call x12, Pallas kernels, call(): pl.pallas_call(kernel, out_shape=out_shape, in_specs=in_specs, out_specs=...  6.67 us
    all_to_all x1, waiting for transfers between devices, exchanged(): return lax.all_to_all(value, axis, 0, 0, tiled=True)  4.35 us
  transfers between devices with their start and end apart: 3, of which 3 were waited for; matrix products, arithmetic and copies ran while one was open for 0% of the time, Pallas kernels for 0%

profile of v3, /device:TPU:1, one launch (start us, length us, event | category | flops | bytes accessed | tf_op | source)
XLA Modules:
  0.0 159.7 jit_solution(16336035935281686455)
XLA Ops:
  1.3 0.0 copy-start.1
  1.3 0.7 copy-done.1
  2.0 1.8 %shard_map.67.own_ref = bf16[512,1024]{1,0:T(8,128)(2,1)S(1)} custom-call(s32[1,1]{1,0:T(1,128)S(6)} %copy.7.total_ref, s32[2,32]{1,0:T(2,128)S(1)} %bitcast.19, bf16[32,128,128]{2,1,0:T(8,128)(2,1)} %bitcast.20), custom_call_target="tpu_custom_call" | custom-call | tf_op jit(solution)/shard_map/pallas_call | solution.py:30
  3.7 0.0 copy-start
  3.7 9.0 %collective-permute-start = (bf16[512,1024]{1,0:T(8,128)(2,1)S(1)}, bf16[512,1024]{1,0:T(8,128)(2,1)S(1)}, u32[]{:S(2)}, u32[]{:S(2)}) collective-permute-start(bf16[512,1024]{1,0:T(8,128)(2,1)S(1)} %shard_map.67.own_ref), channel_id=1, source_target_pairs={{0,1},{1,0},{2,3},{3,2},{4,5},{5,4},{6,7},{7,6},{8,9},{9,8},{10,11... | collective-permute-start | bytes 3145736 | tf_op jit(solution)/shard_map/ppermute | solution.py:220
  12.8 0.0 copy-done
  12.8 0.5 shard_map.68
  13.3 1.7 %collective-permute-done.other_ref = bf16[512,1024]{1,0:T(8,128)(2,1)S(1)} collective-permute-done((bf16[512,1024]{1,0:T(8,128)(2,1)S(1)}, bf16[512,1024]{1,0:T(8,128)(2,1)S(1)}, u32[]{:S(2)}, u32[]{:S(2)}) %collective-permute-start) | collective-permute-done | bytes 1048608 | tf_op jit(solution)/shard_map/ppermute | solution.py:220
  15.0 0.5 shard_map.69
  15.6 21.4 %all_to_all.45.parts_ref = bf16[16,32,128]{2,1,0:T(8,128)(2,1)S(1)} all-to-all(bf16[16,32,128]{2,1,0:T(8,128)(2,1)S(1)} %bitcast.16), channel_id=1, replica_groups=mesh['y'=4,'x'=4,'z'=16,'c'=2] {'z'}, dimensions={0} | all-to-all | bytes 262144 | tf_op jit(solution)/shard_map/all_to_all | solution.py:195
  37.0 13.5 %all_to_all.46 = bf16[16,32,128]{2,1,0:T(8,128)(2,1)S(1)} all-to-all(bf16[16,32,128]{2,1,0:T(8,128)(2,1)S(1)} %get-tuple-element.21), channel_id=1, replica_groups=mesh['y'=4,'x'=4,'z'=16,'c'=2] {'y','x'}, dimensions={0} | all-to-all | bytes 262144 | tf_op jit(solution)/shard_map/all_to_all | solution.py:195
  50.4 0.8 shard_map.71
  51.2 18.2 %all_to_all.47.parts_ref = bf16[16,32,128]{2,1,0:T(8,128)(2,1)S(1)} all-to-all(bf16[16,32,128]{2,1,0:T(8,128)(2,1)S(1)} %bitcast.13), channel_id=1, replica_groups=mesh['y'=4,'x'=4,'z'=16,'c'=2] {'z'}, dimensions={0} | all-to-all | bytes 262144 | tf_op jit(solution)/shard_map/all_to_all | solution.py:195
  69.5 9.9 %all_to_all.48 = bf16[16,32,128]{2,1,0:T(8,128)(2,1)S(1)} all-to-all(bf16[16,32,128]{2,1,0:T(8,128)(2,1)S(1)} %get-tuple-element.24), channel_id=1, replica_groups=mesh['y'=4,'x'=4,'z'=16,'c'=2] {'y','x'}, dimensions={0} | all-to-all | bytes 262144 | tf_op jit(solution)/shard_map/all_to_all | solution.py:195
  79.4 0.8 shard_map.73
  80.2 17.0 %all_to_all.49.parts_ref = bf16[16,32,128]{2,1,0:T(8,128)(2,1)S(1)} all-to-all(bf16[16,32,128]{2,1,0:T(8,128)(2,1)S(1)} %bitcast.15), channel_id=1, replica_groups=mesh['y'=4,'x'=4,'z'=16,'c'=2] {'z'}, dimensions={0} | all-to-all | bytes 262144 | tf_op jit(solution)/shard_map/all_to_all | solution.py:195
  97.2 9.9 %all_to_all.50 = bf16[16,32,128]{2,1,0:T(8,128)(2,1)S(1)} all-to-all(bf16[16,32,128]{2,1,0:T(8,128)(2,1)S(1)} %get-tuple-element.27), channel_id=1, replica_groups=mesh['y'=4,'x'=4,'z'=16,'c'=2] {'y','x'}, dimensions={0} | all-to-all | bytes 262144 | tf_op jit(solution)/shard_map/all_to_all | solution.py:195
  107.1 0.8 shard_map.75
  107.9 15.8 %all_to_all.51.parts_ref = bf16[16,32,128]{2,1,0:T(8,128)(2,1)S(1)} all-to-all(bf16[16,32,128]{2,1,0:T(8,128)(2,1)S(1)} %bitcast.11), channel_id=1, replica_groups=mesh['y'=4,'x'=4,'z'=16,'c'=2] {'z'}, dimensions={0} | all-to-all | bytes 262144 | tf_op jit(solution)/shard_map/all_to_all | solution.py:195
  123.7 0.1 shard_map.76
  123.8 15.3 %all_to_all.52.parts_ref = f32[16,4,128]{2,1,0:T(4,128)S(1)} all-to-all(f32[16,4,128]{2,1,0:T(4,128)S(1)} %get-tuple-element.30), channel_id=1, replica_groups=mesh['y'=4,'x'=4,'z'=16,'c'=2] {'z'}, dimensions={0} | all-to-all | bytes 65536 | tf_op jit(solution)/shard_map/all_to_all | solution.py:195
  139.2 0.7 shard_map.77
  139.8 11.7 %all-to-all-start.8 = ((f32[32,4,128]{2,1,0:T(4,128)}), f32[32,4,128]{2,1,0:T(4,128)S(1)}, u32[]{:S(2)}, u32[]{:S(2)}) async-start(f32[32,4,128]{2,1,0:T(4,128)} %shard_map.77), calls=%async_computation.8 | async-start | bytes 131072 | tf_op jit(solution)/shard_map/all_to_all | solution.py:195
  151.6 2.3 %collective-permute-start.1 = (f32[32,128]{1,0:T(8,128)S(1)}, f32[32,128]{1,0:T(8,128)S(1)}, u32[]{:S(2)}, u32[]{:S(2)}) collective-permute-start(f32[32,128]{1,0:T(8,128)S(1)} %get-tuple-element.32), channel_id=1, source_target_pairs={{0,1},{1,0},{2,3},{3,2},{4,5},{5,4},{6,7},{7,6},{8,9},{9,8},{10,11... | collective-permute-start | bytes 49160 | tf_op jit(solution)/shard_map/ppermute | solution.py:257
  153.8 0.8 collective-permute-done.1.theirs_ref
  154.7 4.4 %all-to-all-done.8.sums_ref = f32[32,4,128]{2,1,0:T(4,128)S(1)} async-done(((f32[32,4,128]{2,1,0:T(4,128)}), f32[32,4,128]{2,1,0:T(4,128)S(1)}, u32[]{:S(2)}, u32[]{:S(2)}) %all-to-all-start.8) | async-done | bytes 65568 | tf_op jit(solution)/shard_map/all_to_all | solution.py:195
  159.0 0.7 shard_map.78
  (3 shorter events, 0.1 us)
Async XLA Ops:
  1.3 0.7 copy-start.1
  3.7 9.0 %copy-start = (s32[128]{0:T(128)S(1)}, s32[128]{0:T(128)}, u32[]{:S(2)}) copy-start(s32[128]{0:T(128)} %param.7) | copy-start | bytes 1540
  3.7 11.3 %collective-permute-start = (bf16[512,1024]{1,0:T(8,128)(2,1)S(1)}, bf16[512,1024]{1,0:T(8,128)(2,1)S(1)}, u32[]{:S(2)}, u32[]{:S(2)}) collective-permute-start(bf16[512,1024]{1,0:T(8,128)(2,1)S(1)} %shard_map.67.own_ref), channel_id=1, source_target_pairs={{0,1},{1,0},{2,3},{3,2},{4,5},{5,4},{6,7},{7,6},{8,9},{9,8},{10,11... | collective-permute-start | bytes 3145736 | tf_op jit(solution)/shard_map/ppermute | solution.py:220
  139.8 19.2 %all-to-all-start.8 = ((f32[32,4,128]{2,1,0:T(4,128)}), f32[32,4,128]{2,1,0:T(4,128)S(1)}, u32[]{:S(2)}, u32[]{:S(2)}) async-start(f32[32,4,128]{2,1,0:T(4,128)} %shard_map.77), calls=%async_computation.8 | async-start | bytes 131072 | tf_op jit(solution)/shard_map/all_to_all | solution.py:195
  151.6 3.1 %collective-permute-start.1 = (f32[32,128]{1,0:T(8,128)S(1)}, f32[32,128]{1,0:T(8,128)S(1)}, u32[]{:S(2)}, u32[]{:S(2)}) collective-permute-start(f32[32,128]{1,0:T(8,128)S(1)} %get-tuple-element.32), channel_id=1, source_target_pairs={{0,1},{1,0},{2,3},{3,2},{4,5},{5,4},{6,7},{7,6},{8,9},{9,8},{10,11... | collective-permute-start | bytes 49160 | tf_op jit(solution)/shard_map/ppermute | solution.py:257

commit v4 on v3

--- a/solution.py
+++ b/solution.py
@@ -14,7 +14,6 @@
 LEVELS = 4
 TILE = 128
 GRANT = 8 << 20
-BUILD_GRANT = 209 << 18
 CHUNKS = 4
 Y, X, Z, C = "y", "x", "z", "c"
 ROW = (Y, X)
@@ -26,26 +25,28 @@
 F32 = jnp.float32
 
 
-def call(kernel, out_shape, in_specs, *operands, scratch=(), grant=GRANT):
+def call(kernel, out_shape, in_specs, *operands, scratch=()):
     return pl.pallas_call(
         kernel,
         out_shape=out_shape,
         in_specs=in_specs,
         out_specs=jax.tree.map(lambda _: VMEM, out_shape),
         scratch_shapes=scratch,
-        compiler_params=pltpu.CompilerParams(vmem_limit_bytes=grant),
+        compiler_params=pltpu.CompilerParams(vmem_limit_bytes=GRANT),
     )(*operands)
 
 
-def build_kernel(total_ref, pos_ref, tiles_any, dense_ref, tiles_ref, tile_sems):
+def build_kernel(total_ref, pos_hbm, tiles_hbm, dense_ref, pos_ref, tiles_ref, pos_sem, tile_sems):
     columns = dense_ref.shape[1] // 2
     core = lax.axis_index(C)
     slots = tiles_ref.shape[0]
     step = slots // CHUNKS
+    pos_copy = pltpu.make_async_copy(pos_hbm, pos_ref, pos_sem)
+    pos_copy.start()
     tile_copies = []
     for chunk in range(CHUNKS):
         part = pl.ds(chunk * step, step)
-        tile_copies.append(pltpu.make_async_copy(tiles_any.at[part], tiles_ref.at[part], tile_sems.at[chunk]))
+        tile_copies.append(pltpu.make_async_copy(tiles_hbm.at[part], tiles_ref.at[part], tile_sems.at[chunk]))
         tile_copies[-1].start()
     dense_ref[...] = jnp.zeros_like(dense_ref)
 
@@ -59,6 +60,7 @@
                 dense_ref[pl.ds(rows, PV), pl.ds(lanes, TILE)] = tiles_ref[slot, pl.ds(first, PV), :]
         return carry
 
+    pos_copy.wait()
     for chunk in range(CHUNKS):
         tile_copies[chunk].wait()
         lax.fori_loop(chunk * step, jnp.minimum(total_ref[0, 0], (chunk + 1) * step), place, 0)
@@ -207,13 +209,14 @@
     own = call(
         build_kernel,
         bf(dests, 2 * sources),
-        [SMEM, SMEM, ANY],
+        [SMEM, ANY, ANY],
         tile_total,
-        tile_pos[0, 0],
-        tile_weights[0, 0],
-        grant=BUILD_GRANT,
+        pltpu.with_memory_space_constraint(tile_pos[0, 0], pltpu.HBM),
+        pltpu.with_memory_space_constraint(tile_weights[0, 0], pltpu.HBM),
         scratch=[
+            pltpu.SMEM((2, slots), jnp.int32),
             pltpu.VMEM((slots, TILE, TILE), BF),
+            pltpu.SemaphoreType.DMA,
             pltpu.SemaphoreType.DMA((CHUNKS,)),
         ],
     )

time: 160 us -> 159 us (level)
  no operation moved by 1% of the time
where the time goes in v4:
time: 159 us; the launch traced here: 158 us
  blocking collectives  121 us (76%)
  starting transfers between devices  22.6 us (14%)
  waiting for transfers between devices  6.91 us (4%)
  Pallas kernels  6.38 us (4%)
    all_to_all x8, blocking collectives, exchanged(): return lax.all_to_all(value, axis, 0, 0, tiled=True)  121 us
    all_to_all x1, starting transfers between devices, exchanged(): return lax.all_to_all(value, axis, 0, 0, tiled=True)  11.7 us
    ppermute x1, starting transfers between devices, local(): other = lax.ppermute(own, C, swap)  8.62 us
    pallas_call x12, Pallas kernels, call(): pl.pallas_call(kernel, out_shape=out_shape, in_specs=in_specs, out_specs=...  6.38 us
    all_to_all x1, waiting for transfers between devices, exchanged(): return lax.all_to_all(value, axis, 0, 0, tiled=True)  4.35 us
  transfers between devices with their start and end apart: 3, of which 3 were waited for; matrix products, arithmetic and copies ran while one was open for 0% of the time, Pallas kernels for 0%

profile of v4, /device:TPU:1, one launch (start us, length us, event | category | flops | bytes accessed | tf_op | source)
XLA Modules:
  0.0 158.5 jit_solution(940861256746914709)
XLA Ops:
  1.3 1.5 shard_map.67.own_ref
  2.8 0.0 copy-start
  2.8 8.6 %collective-permute-start = (bf16[512,1024]{1,0:T(8,128)(2,1)S(1)}, bf16[512,1024]{1,0:T(8,128)(2,1)S(1)}, u32[]{:S(2)}, u32[]{:S(2)}) collective-permute-start(bf16[512,1024]{1,0:T(8,128)(2,1)S(1)} %shard_map.67.own_ref), channel_id=1, source_target_pairs={{0,1},{1,0},{2,3},{3,2},{4,5},{5,4},{6,7},{7,6},{8,9},{9,8},{10,11... | collective-permute-start | bytes 3145736 | tf_op jit(solution)/shard_map/ppermute | solution.py:223
  11.4 0.0 copy-done
  11.4 0.5 shard_map.68
  11.9 1.7 %collective-permute-done.other_ref = bf16[512,1024]{1,0:T(8,128)(2,1)S(1)} collective-permute-done((bf16[512,1024]{1,0:T(8,128)(2,1)S(1)}, bf16[512,1024]{1,0:T(8,128)(2,1)S(1)}, u32[]{:S(2)}, u32[]{:S(2)}) %collective-permute-start) | collective-permute-done | bytes 1048608 | tf_op jit(solution)/shard_map/ppermute | solution.py:223
  13.7 0.5 shard_map.69
  14.2 21.4 %all_to_all.45.parts_ref = bf16[16,32,128]{2,1,0:T(8,128)(2,1)S(1)} all-to-all(bf16[16,32,128]{2,1,0:T(8,128)(2,1)S(1)} %bitcast.16), channel_id=1, replica_groups=mesh['y'=4,'x'=4,'z'=16,'c'=2] {'z'}, dimensions={0} | all-to-all | bytes 262144 | tf_op jit(solution)/shard_map/all_to_all | solution.py:197
  35.6 13.6 %all_to_all.46 = bf16[16,32,128]{2,1,0:T(8,128)(2,1)S(1)} all-to-all(bf16[16,32,128]{2,1,0:T(8,128)(2,1)S(1)} %get-tuple-element.21), channel_id=1, replica_groups=mesh['y'=4,'x'=4,'z'=16,'c'=2] {'y','x'}, dimensions={0} | all-to-all | bytes 262144 | tf_op jit(solution)/shard_map/all_to_all | solution.py:197
  49.2 0.8 shard_map.71
  50.0 18.2 %all_to_all.47.parts_ref = bf16[16,32,128]{2,1,0:T(8,128)(2,1)S(1)} all-to-all(bf16[16,32,128]{2,1,0:T(8,128)(2,1)S(1)} %bitcast.13), channel_id=1, replica_groups=mesh['y'=4,'x'=4,'z'=16,'c'=2] {'z'}, dimensions={0} | all-to-all | bytes 262144 | tf_op jit(solution)/shard_map/all_to_all | solution.py:197
  68.2 9.9 %all_to_all.48 = bf16[16,32,128]{2,1,0:T(8,128)(2,1)S(1)} all-to-all(bf16[16,32,128]{2,1,0:T(8,128)(2,1)S(1)} %get-tuple-element.24), channel_id=1, replica_groups=mesh['y'=4,'x'=4,'z'=16,'c'=2] {'y','x'}, dimensions={0} | all-to-all | bytes 262144 | tf_op jit(solution)/shard_map/all_to_all | solution.py:197
  78.2 0.8 shard_map.73
  79.0 17.0 %all_to_all.49.parts_ref = bf16[16,32,128]{2,1,0:T(8,128)(2,1)S(1)} all-to-all(bf16[16,32,128]{2,1,0:T(8,128)(2,1)S(1)} %bitcast.15), channel_id=1, replica_groups=mesh['y'=4,'x'=4,'z'=16,'c'=2] {'z'}, dimensions={0} | all-to-all | bytes 262144 | tf_op jit(solution)/shard_map/all_to_all | solution.py:197
  96.0 9.9 %all_to_all.50 = bf16[16,32,128]{2,1,0:T(8,128)(2,1)S(1)} all-to-all(bf16[16,32,128]{2,1,0:T(8,128)(2,1)S(1)} %get-tuple-element.27), channel_id=1, replica_groups=mesh['y'=4,'x'=4,'z'=16,'c'=2] {'y','x'}, dimensions={0} | all-to-all | bytes 262144 | tf_op jit(solution)/shard_map/all_to_all | solution.py:197
  105.9 0.8 shard_map.75
  106.7 15.8 %all_to_all.51.parts_ref = bf16[16,32,128]{2,1,0:T(8,128)(2,1)S(1)} all-to-all(bf16[16,32,128]{2,1,0:T(8,128)(2,1)S(1)} %bitcast.11), channel_id=1, replica_groups=mesh['y'=4,'x'=4,'z'=16,'c'=2] {'z'}, dimensions={0} | all-to-all | bytes 262144 | tf_op jit(solution)/shard_map/all_to_all | solution.py:197
  122.5 0.1 shard_map.76
  122.6 15.3 %all_to_all.52.parts_ref = f32[16,4,128]{2,1,0:T(4,128)S(1)} all-to-all(f32[16,4,128]{2,1,0:T(4,128)S(1)} %get-tuple-element.30), channel_id=1, replica_groups=mesh['y'=4,'x'=4,'z'=16,'c'=2] {'z'}, dimensions={0} | all-to-all | bytes 65536 | tf_op jit(solution)/shard_map/all_to_all | solution.py:197
  137.9 0.6 shard_map.77
  138.6 11.7 %all-to-all-start.8 = ((f32[32,4,128]{2,1,0:T(4,128)}), f32[32,4,128]{2,1,0:T(4,128)S(1)}, u32[]{:S(2)}, u32[]{:S(2)}) async-start(f32[32,4,128]{2,1,0:T(4,128)} %shard_map.77), calls=%async_computation.8 | async-start | bytes 131072 | tf_op jit(solution)/shard_map/all_to_all | solution.py:197
  150.3 2.3 %collective-permute-start.1 = (f32[32,128]{1,0:T(8,128)S(1)}, f32[32,128]{1,0:T(8,128)S(1)}, u32[]{:S(2)}, u32[]{:S(2)}) collective-permute-start(f32[32,128]{1,0:T(8,128)S(1)} %get-tuple-element.32), channel_id=1, source_target_pairs={{0,1},{1,0},{2,3},{3,2},{4,5},{5,4},{6,7},{7,6},{8,9},{9,8},{10,11... | collective-permute-start | bytes 49160 | tf_op jit(solution)/shard_map/ppermute | solution.py:260
  152.6 0.8 collective-permute-done.1.theirs_ref
  153.4 4.4 %all-to-all-done.8.sums_ref = f32[32,4,128]{2,1,0:T(4,128)S(1)} async-done(((f32[32,4,128]{2,1,0:T(4,128)}), f32[32,4,128]{2,1,0:T(4,128)S(1)}, u32[]{:S(2)}, u32[]{:S(2)}) %all-to-all-start.8) | async-done | bytes 65568 | tf_op jit(solution)/shard_map/all_to_all | solution.py:197
  157.8 0.7 shard_map.78
  (3 shorter events, 0.1 us)
Async XLA Ops:
  2.8 8.6 %copy-start = (s32[128]{0:T(128)S(1)}, s32[128]{0:T(128)}, u32[]{:S(2)}) copy-start(s32[128]{0:T(128)} %param.7) | copy-start | bytes 1540
  2.8 10.9 %collective-permute-start = (bf16[512,1024]{1,0:T(8,128)(2,1)S(1)}, bf16[512,1024]{1,0:T(8,128)(2,1)S(1)}, u32[]{:S(2)}, u32[]{:S(2)}) collective-permute-start(bf16[512,1024]{1,0:T(8,128)(2,1)S(1)} %shard_map.67.own_ref), channel_id=1, source_target_pairs={{0,1},{1,0},{2,3},{3,2},{4,5},{5,4},{6,7},{7,6},{8,9},{9,8},{10,11... | collective-permute-start | bytes 3145736 | tf_op jit(solution)/shard_map/ppermute | solution.py:223
  138.6 19.2 %all-to-all-start.8 = ((f32[32,4,128]{2,1,0:T(4,128)}), f32[32,4,128]{2,1,0:T(4,128)S(1)}, u32[]{:S(2)}, u32[]{:S(2)}) async-start(f32[32,4,128]{2,1,0:T(4,128)} %shard_map.77), calls=%async_computation.8 | async-start | bytes 131072 | tf_op jit(solution)/shard_map/all_to_all | solution.py:197
  150.3 3.1 %collective-permute-start.1 = (f32[32,128]{1,0:T(8,128)S(1)}, f32[32,128]{1,0:T(8,128)S(1)}, u32[]{:S(2)}, u32[]{:S(2)}) collective-permute-start(f32[32,128]{1,0:T(8,128)S(1)} %get-tuple-element.32), channel_id=1, source_target_pairs={{0,1},{1,0},{2,3},{3,2},{4,5},{5,4},{6,7},{7,6},{8,9},{9,8},{10,11... | collective-permute-start | bytes 49160 | tf_op jit(solution)/shard_map/ppermute | solution.py:260

commit v5 on v4

--- a/solution.py
+++ b/solution.py
@@ -36,28 +36,48 @@
     )(*operands)
 
 
-def build_kernel(total_ref, pos_hbm, tiles_hbm, dense_ref, pos_ref, tiles_ref, pos_sem, tile_sems):
-    columns = dense_ref.shape[1] // 2
+def start_kernel(
+    row_block,
+    total_ref,
+    pos_hbm,
+    tiles_hbm,
+    roots_hbm,
+    near_ref,
+    far_ref,
+    mine_ref,
+    theirs_ref,
+    hop_ref,
+    kept_ref,
+    pos_ref,
+    tiles_ref,
+    roots_ref,
+    pos_sem,
+    roots_sem,
+    tile_sems,
+):
     core = lax.axis_index(C)
     slots = tiles_ref.shape[0]
     step = slots // CHUNKS
     pos_copy = pltpu.make_async_copy(pos_hbm, pos_ref, pos_sem)
     pos_copy.start()
+    roots_copy = pltpu.make_async_copy(roots_hbm, roots_ref, roots_sem)
+    roots_copy.start()
     tile_copies = []
     for chunk in range(CHUNKS):
         part = pl.ds(chunk * step, step)
         tile_copies.append(pltpu.make_async_copy(tiles_hbm.at[part], tiles_ref.at[part], tile_sems.at[chunk]))
         tile_copies[-1].start()
-    dense_ref[...] = jnp.zeros_like(dense_ref)
+    for block_ref in (near_ref, far_ref):
+        block_ref[...] = jnp.zeros_like(block_ref)
 
     def place(slot, carry):
         dest, source = pos_ref[0, slot], pos_ref[1, slot]
         for part in range(2):
-            for half in range(2):
+            for half, block_ref in enumerate((near_ref, far_ref)):
                 first = pl.multiple_of(part * 2 * PV + (half ^ core) * PV, PV)
                 rows = pl.multiple_of(dest * 2 * PV + part * PV, PV)
-                lanes = pl.multiple_of(half * columns + source * TILE, TILE)
-                dense_ref[pl.ds(rows, PV), pl.ds(lanes, TILE)] = tiles_ref[slot, pl.ds(first, PV), :]
+                lanes = pl.multiple_of(source * TILE, TILE)
+                block_ref[pl.ds(rows, PV), pl.ds(lanes, TILE)] = tiles_ref[slot, pl.ds(first, PV), :]
         return carry
 
     pos_copy.wait()
@@ -65,6 +85,9 @@
         tile_copies[chunk].wait()
         lax.fori_loop(chunk * step, jnp.minimum(total_ref[0, 0], (chunk + 1) * step), place, 0)
 
+    roots_copy.wait()
+    first_products(row_block, roots_ref, near_ref, far_ref, mine_ref, theirs_ref, hop_ref, kept_ref)
+
 
 def left_half(shape):
     return lax.broadcasted_iota(jnp.int32, shape, len(shape) - 1) < HALF
@@ -72,61 +95,55 @@
 
 def own_roots(roots_ref):
     roots = roots_ref[...]
-    turned = pltpu.roll(roots, HALF, 1)
-    return jnp.where(left_half(roots.shape) == (lax.axis_index(C) == 0), roots, turned)
-
-
-def times(ref, half, value):
-    rows = value.shape[0]
-    return jnp.dot(ref[:, half * rows : (half + 1) * rows], value.astype(BF), preferred_element_type=F32)
-
-
-def own_products(own_ref, front, turned):
+    return jnp.where(lax.axis_index(C) == 0, roots, pltpu.roll(roots, HALF, 1))
+
+
+def times(ref, value):
+    return jnp.dot(ref[...], value.astype(BF), preferred_element_type=F32)
+
+
+def own_products(near_ref, far_ref, front, turned):
     left = left_half(front.shape)
     zero = jnp.zeros_like(front)
-    return times(own_ref, 0, jnp.where(left, front, zero)) + times(own_ref, 1, jnp.where(left, zero, turned))
-
-
-def other_products(other_ref, front, turned):
+    return times(near_ref, jnp.where(left, front, zero)) + times(far_ref, jnp.where(left, zero, turned))
+
+
+def other_products(near_ref, far_ref, front, turned):
     left = left_half(front.shape)
     zero = jnp.zeros_like(front)
-    return times(other_ref, 0, jnp.where(left, zero, front)) + times(other_ref, 1, jnp.where(left, turned, zero))
-
-
-def root_front(row_block, roots_ref, sources):
+    return times(near_ref, jnp.where(left, zero, front)) + times(far_ref, jnp.where(left, turned, zero))
+
+
+def first_products(row_block, roots_ref, near_ref, far_ref, mine_ref, theirs_ref, hop_ref, kept_ref):
     core, pair = lax.axis_index(C), lax.axis_index(Z) * 2 * PV
     base_own, base_other = pair + core * PV, pair + (1 - core) * PV
     roots = own_roots(roots_ref)
-    shape = (sources, ROOTS)
+    turned = pltpu.roll(roots, HALF, 1)
+    shape = (near_ref.shape[1], ROOTS)
     row = lax.broadcasted_iota(jnp.int32, shape, 0)
-    left = left_half(shape)
-    vertex = (row // PV) * row_block + row % PV
-    front = (vertex + jnp.where(left, base_own, base_other) == roots).astype(F32)
-    turned = (vertex + jnp.where(left, base_other, base_own) == roots).astype(F32)
-    return front, turned
-
-
-def first_own_kernel(row_block, roots_ref, own_ref, part_ref, hop_ref, kept_ref):
-    front, turned = root_front(row_block, roots_ref, own_ref.shape[1] // 2)
-    part_ref[...] = own_products(own_ref, front, turned)
-    core, pair = lax.axis_index(C), lax.axis_index(Z) * 2 * PV
-    base_own, base_other = pair + core * PV, pair + (1 - core) * PV
+    vertex = (row // PV) * row_block + row % PV + base_own
+    near = times(near_ref, (vertex == roots).astype(F32))
+    far = times(far_ref, (vertex == turned).astype(F32))
+    left = left_half(near.shape)
+    mine_ref[...] = jnp.where(left, near, far).astype(BF)
+    theirs_ref[...] = jnp.where(left, far, near).astype(BF)
     state = hop_ref.shape
+    left = left_half(state)
     vertex = lax.broadcasted_iota(jnp.int32, state, 0) + lax.axis_index(ROW) * row_block
-    is_root = vertex + jnp.where(left_half(state), base_own, base_other) == own_roots(roots_ref)
+    is_root = vertex + jnp.where(left, base_own, base_other) == jnp.where(left, roots, turned)
     kept_ref[...] = is_root.astype(F32)
     hop_ref[...] = jnp.where(is_root, 0, LEVELS + 1)
 
 
-def first_other_kernel(row_block, roots_ref, other_ref, part_ref, sent_ref):
-    front, turned = root_front(row_block, roots_ref, other_ref.shape[1] // 2)
-    sent_ref[...] = (part_ref[...] + other_products(other_ref, front, turned)).astype(BF)
-
-
-def level_kernel(front_ref, own_ref, other_ref, sent_ref):
+def add_kernel(mine_ref, both_ref, sent_ref):
+    sent_ref[...] = (mine_ref[...].astype(F32) + both_ref[1 - lax.axis_index(C)].astype(F32)).astype(BF)
+
+
+def level_kernel(front_ref, own_near, own_far, other_near, other_far, sent_ref):
     front = front_ref[...].astype(F32)
     turned = pltpu.roll(front, HALF, 1)
-    total = own_products(own_ref, front, turned) + other_products(other_ref, front, turned)
+    total = own_products(own_near, own_far, front, turned)
+    total += other_products(other_near, other_far, front, turned)
     sent_ref[...] = total.astype(BF)
 
 
@@ -206,36 +223,27 @@
     swap = [(0, 1), (1, 0)]
 
     slots = tile_weights.shape[2]
-    own = call(
-        build_kernel,
-        bf(dests, 2 * sources),
-        [SMEM, ANY, ANY],
+    held = lambda value: pltpu.with_memory_space_constraint(value, pltpu.HBM)
+    near, far, mine, theirs, hop, kept = call(
+        functools.partial(start_kernel, row_block),
+        (bf(dests, sources), bf(dests, sources), bf(dests, ROOTS), bf(dests, ROOTS), hops, f32(PV, ROOTS)),
+        [SMEM, ANY, ANY, ANY],
         tile_total,
-        pltpu.with_memory_space_constraint(tile_pos[0, 0], pltpu.HBM),
-        pltpu.with_memory_space_constraint(tile_weights[0, 0], pltpu.HBM),
+        held(tile_pos[0, 0]),
+        held(tile_weights[0, 0]),
+        held(root_ids[None]),
         scratch=[
             pltpu.SMEM((2, slots), jnp.int32),
             pltpu.VMEM((slots, TILE, TILE), BF),
+            pltpu.VMEM((1, ROOTS), jnp.int32),
+            pltpu.SemaphoreType.DMA,
             pltpu.SemaphoreType.DMA,
             pltpu.SemaphoreType.DMA((CHUNKS,)),
         ],
     )
-    other = lax.ppermute(own, C, swap)
-    part, hop, kept = call(
-        functools.partial(first_own_kernel, row_block),
-        (f32(dests, ROOTS), hops, f32(PV, ROOTS)),
-        [VMEM] * 2,
-        root_ids[None],
-        own,
-    )
-    sent = call(
-        functools.partial(first_other_kernel, row_block),
-        bf(dests, ROOTS),
-        [VMEM] * 3,
-        root_ids[None],
-        other,
-        part,
-    )
+    both = lax.all_gather(theirs, C)
+    blocks = (near, far, lax.ppermute(near, C, swap), lax.ppermute(far, C, swap))
+    sent = call(add_kernel, bf(dests, ROOTS), [VMEM] * 2, mine, both)
     for level in range(1, LEVELS):
         parts = exchanged(sent.reshape(z_all, PV, ROOTS), Z)
         hop, kept, front = call(
@@ -247,7 +255,7 @@
             kept,
         )
         front = exchanged(front, ROW).reshape(sources, ROOTS)
-        sent = call(level_kernel, bf(dests, ROOTS), [VMEM] * 3, front, own, other)
+        sent = call(level_kernel, bf(dests, ROOTS), [VMEM] * 5, front, *blocks)
     parts = exchanged(sent.reshape(z_all, PV, ROOTS), Z)
     mine, theirs, sums = call(
         last_kernel,

time: 159 us -> 158 us (level)
  blocking collectives: 121 us -> 94.7 us
  waiting for transfers between devices: 6.91 us -> 19.6 us
  starting transfers between devices: 22.6 us -> 34.9 us
    all_to_all x8 -> x6, blocking collectives: 121 us -> 86.2 us  [exchanged(): return lax.all_to_all(value, axis, 0, 0, tiled=True)]
    all_to_all x1 -> x3, starting transfers between devices: 11.7 us -> 28.1 us  [exchanged(): return lax.all_to_all(value, axis, 0, 0, tiled=True)]
    all_to_all x1 -> x3, waiting for transfers between devices: 4.35 us -> 18.8 us  [exchanged(): return lax.all_to_all(value, axis, 0, 0, tiled=True)]
    all_gather x0 -> x1, blocking collectives: none -> 8.51 us  [local(): both = lax.all_gather(theirs, C)]
    ppermute x1 -> x2, starting transfers between devices: 8.62 us -> 4.47 us  [the longest x1 2.55 us: local(): lax.ppermute(near, C, swap)]
    ppermute x1 -> x2, waiting for transfers between devices: 1.74 us -> 0.01 us  [the longest x1 0.01 us: local(): lax.ppermute(near, C, swap)]
    pallas_call x12 -> x11, Pallas kernels: 6.38 us -> 7.04 us  [call(): pl.pallas_call(kernel, out_shape=out_shape, in_specs=in_specs, out_specs=...]
  transfers between devices with their start and end apart: 3 -> 6, of which waited for: 3 -> 4; matrix products, arithmetic and copies ran while one was open for 0% -> 0% of each run, Pallas kernels for 0% -> 0%
where the time goes in v5:
time: 158 us
  blocking collectives  94.7 us (60%)
  starting transfers between devices  34.9 us (22%)
  waiting for transfers between devices  19.6 us (12%)
  Pallas kernels  7.04 us (4%)
    all_to_all x6, blocking collectives, exchanged(): return lax.all_to_all(value, axis, 0, 0, tiled=True)  86.2 us
    all_to_all x3, starting transfers between devices, exchanged(): return lax.all_to_all(value, axis, 0, 0, tiled=True)  28.1 us
    all_to_all x3, waiting for transfers between devices, exchanged(): return lax.all_to_all(value, axis, 0, 0, tiled=True)  18.8 us
    all_gather x1, blocking collectives, local(): both = lax.all_gather(theirs, C)  8.51 us
    pallas_call x11, Pallas kernels, call(): pl.pallas_call(kernel, out_shape=out_shape, in_specs=in_specs, out_specs=...  7.04 us
  transfers between devices with their start and end apart: 6, of which 4 were waited for; matrix products, arithmetic and copies ran while one was open for 0% of the time, Pallas kernels for 0%

profile of v5, /device:TPU:1, one launch (start us, length us, event | category | flops | bytes accessed | tf_op | source)
XLA Modules:
  0.0 157.7 jit_solution(17662389493703499731)
XLA Ops:
  1.3 1.8 %shard_map.67 = (bf16[512,512]{1,0:T(8,128)(2,1)S(1)}, bf16[512,512]{1,0:T(8,128)(2,1)S(1)}, bf16[512,128]{1,0:T(8,128)(2,1)S(1)}, bf16[512,128]{1,0:T(8,128)(2,...) custom-call(s32[1,1]{1,0:T(1,128)S(6)} %copy.7.total_ref, s32[2,32]{1,0:T(2,128)} %bitcast.19, ...), custom_call_target="tpu_custom_call" | custom-call | tf_op jit(solution)/shard_map/pallas_call | solution.py:29
  3.1 8.5 %all-gather = bf16[1024,128]{1,0:T(8,128)(2,1)S(1)} all-gather(bf16[512,128]{1,0:T(8,128)(2,1)S(1)} %get-tuple-element.22), channel_id=2, replica_groups=mesh['y'=4,'x'=4,'z'=16,'c'=2] {'c'}, dimensions={0}, use_global_device_ids=true | all-gather | bytes 393216 | tf_op jit(solution)/shard_map/all_gather | solution.py:244
  11.6 0.7 shard_map.68
  12.3 9.6 %all-to-all-start = ((bf16[16,32,128]{2,1,0:T(8,128)(2,1)}), bf16[16,32,128]{2,1,0:T(8,128)(2,1)S(1)}, u32[]{:S(2)}, u32[]{:S(2)}) async-start(bf16[16,32,128]{2,1,0:T(8,128)(2,1)} %bitcast.4), calls=%async_computation | async-start | bytes 262144 | tf_op jit(solution)/shard_map/all_to_all | solution.py:214
  21.9 2.6 %collective-permute-start = (bf16[512,512]{1,0:T(8,128)(2,1)S(1)}, bf16[512,512]{1,0:T(8,128)(2,1)S(1)}, u32[]{:S(2)}, u32[]{:S(2)}) collective-permute-start(bf16[512,512]{1,0:T(8,128)(2,1)S(1)} %get-tuple-element.26.own_near), channel_id=1, source_target_pairs={{0,1},{1,0},{2,3},{3,2},{4,5},{5,4},{6,7},{7,6},{8,9},{9,8},{10,11... | collective-permute-start | bytes 1572872 | tf_op jit(solution)/shard_map/ppermute | solution.py:245
  24.4 1.9 %collective-permute-start.1 = (bf16[512,512]{1,0:T(8,128)(2,1)S(1)}, bf16[512,512]{1,0:T(8,128)(2,1)S(1)}, u32[]{:S(2)}, u32[]{:S(2)}) collective-permute-start(bf16[512,512]{1,0:T(8,128)(2,1)S(1)} %get-tuple-element.27.own_far), channel_id=1, source_target_pairs={{0,1},{1,0},{2,3},{3,2},{4,5},{5,4},{6,7},{7,6},{8,9},{9,8},{10,11... | collective-permute-start | bytes 1572872 | tf_op jit(solution)/shard_map/ppermute | solution.py:245
  26.4 7.7 %all-to-all-done.parts_ref = bf16[16,32,128]{2,1,0:T(8,128)(2,1)S(1)} async-done(((bf16[16,32,128]{2,1,0:T(8,128)(2,1)}), bf16[16,32,128]{2,1,0:T(8,128)(2,1)S(1)}, u32[]{:S(2)}, u32[]{:S(2)}) %all-to-all-start) | async-done | bytes 131104 | tf_op jit(solution)/shard_map/all_to_all | solution.py:214
  34.0 0.7 shard_map.69
  34.7 6.8 %all-to-all-start.1 = ((bf16[16,32,128]{2,1,0:T(8,128)(2,1)}), bf16[16,32,128]{2,1,0:T(8,128)(2,1)S(1)}, u32[]{:S(2)}, u32[]{:S(2)}) async-start(bf16[16,32,128]{2,1,0:T(8,128)(2,1)} %get-tuple-element.25), calls=%async_computation.1 | async-start | bytes 262144 | tf_op jit(solution)/shard_map/all_to_all | solution.py:214
  41.5 0.0 collective-permute-done.other_near
  41.5 0.0 collective-permute-done.1.other_far
  41.5 6.8 %all-to-all-done.1 = bf16[16,32,128]{2,1,0:T(8,128)(2,1)S(1)} async-done(((bf16[16,32,128]{2,1,0:T(8,128)(2,1)}), bf16[16,32,128]{2,1,0:T(8,128)(2,1)S(1)}, u32[]{:S(2)}, u32[]{:S(2)}) %all-to-all-start.1) | async-done | bytes 131104 | tf_op jit(solution)/shard_map/all_to_all | solution.py:214
  48.4 0.8 shard_map.70
  49.1 18.2 %all_to_all.45.parts_ref = bf16[16,32,128]{2,1,0:T(8,128)(2,1)S(1)} all-to-all(bf16[16,32,128]{2,1,0:T(8,128)(2,1)S(1)} %bitcast.15), channel_id=1, replica_groups=mesh['y'=4,'x'=4,'z'=16,'c'=2] {'z'}, dimensions={0} | all-to-all | bytes 262144 | tf_op jit(solution)/shard_map/all_to_all | solution.py:214
  67.4 9.9 %all_to_all.46 = bf16[16,32,128]{2,1,0:T(8,128)(2,1)S(1)} all-to-all(bf16[16,32,128]{2,1,0:T(8,128)(2,1)S(1)} %get-tuple-element.30), channel_id=1, replica_groups=mesh['y'=4,'x'=4,'z'=16,'c'=2] {'y','x'}, dimensions={0} | all-to-all | bytes 262144 | tf_op jit(solution)/shard_map/all_to_all | solution.py:214
  77.3 0.8 shard_map.72
  78.1 16.9 %all_to_all.47.parts_ref = bf16[16,32,128]{2,1,0:T(8,128)(2,1)S(1)} all-to-all(bf16[16,32,128]{2,1,0:T(8,128)(2,1)S(1)} %bitcast.17), channel_id=1, replica_groups=mesh['y'=4,'x'=4,'z'=16,'c'=2] {'z'}, dimensions={0} | all-to-all | bytes 262144 | tf_op jit(solution)/shard_map/all_to_all | solution.py:214
  95.1 9.9 %all_to_all.48 = bf16[16,32,128]{2,1,0:T(8,128)(2,1)S(1)} all-to-all(bf16[16,32,128]{2,1,0:T(8,128)(2,1)S(1)} %get-tuple-element.33), channel_id=1, replica_groups=mesh['y'=4,'x'=4,'z'=16,'c'=2] {'y','x'}, dimensions={0} | all-to-all | bytes 262144 | tf_op jit(solution)/shard_map/all_to_all | solution.py:214
  105.0 0.8 shard_map.74
  105.8 15.8 %all_to_all.49.parts_ref = bf16[16,32,128]{2,1,0:T(8,128)(2,1)S(1)} all-to-all(bf16[16,32,128]{2,1,0:T(8,128)(2,1)S(1)} %bitcast.14), channel_id=1, replica_groups=mesh['y'=4,'x'=4,'z'=16,'c'=2] {'z'}, dimensions={0} | all-to-all | bytes 262144 | tf_op jit(solution)/shard_map/all_to_all | solution.py:214
  121.6 0.1 shard_map.75
  121.7 15.4 %all_to_all.50.parts_ref = f32[16,4,128]{2,1,0:T(4,128)S(1)} all-to-all(f32[16,4,128]{2,1,0:T(4,128)S(1)} %get-tuple-element.36), channel_id=1, replica_groups=mesh['y'=4,'x'=4,'z'=16,'c'=2] {'z'}, dimensions={0} | all-to-all | bytes 65536 | tf_op jit(solution)/shard_map/all_to_all | solution.py:214
  137.1 0.6 shard_map.76
  137.8 11.8 %all-to-all-start.8 = ((f32[32,4,128]{2,1,0:T(4,128)}), f32[32,4,128]{2,1,0:T(4,128)S(1)}, u32[]{:S(2)}, u32[]{:S(2)}) async-start(f32[32,4,128]{2,1,0:T(4,128)} %shard_map.76), calls=%async_computation.8 | async-start | bytes 131072 | tf_op jit(solution)/shard_map/all_to_all | solution.py:214
  149.5 2.3 %collective-permute-start.2 = (f32[32,128]{1,0:T(8,128)S(1)}, f32[32,128]{1,0:T(8,128)S(1)}, u32[]{:S(2)}, u32[]{:S(2)}) collective-permute-start(f32[32,128]{1,0:T(8,128)S(1)} %get-tuple-element.38), channel_id=1, source_target_pairs={{0,1},{1,0},{2,3},{3,2},{4,5},{5,4},{6,7},{7,6},{8,9},{9,8},{10,11... | collective-permute-start | bytes 49160 | tf_op jit(solution)/shard_map/ppermute | solution.py:268
  151.8 0.8 collective-permute-done.2.theirs_ref
  152.6 4.4 %all-to-all-done.8.sums_ref = f32[32,4,128]{2,1,0:T(4,128)S(1)} async-done(((f32[32,4,128]{2,1,0:T(4,128)}), f32[32,4,128]{2,1,0:T(4,128)S(1)}, u32[]{:S(2)}, u32[]{:S(2)}) %all-to-all-start.8) | async-done | bytes 65568 | tf_op jit(solution)/shard_map/all_to_all | solution.py:214
  156.9 0.7 shard_map.77
  (2 shorter events, 0.1 us)
Async XLA Ops:
  12.3 21.7 %all-to-all-start = ((bf16[16,32,128]{2,1,0:T(8,128)(2,1)}), bf16[16,32,128]{2,1,0:T(8,128)(2,1)S(1)}, u32[]{:S(2)}, u32[]{:S(2)}) async-start(bf16[16,32,128]{2,1,0:T(8,128)(2,1)} %bitcast.4), calls=%async_computation | async-start | bytes 262144 | tf_op jit(solution)/shard_map/all_to_all | solution.py:214
  21.9 19.7 %collective-permute-start = (bf16[512,512]{1,0:T(8,128)(2,1)S(1)}, bf16[512,512]{1,0:T(8,128)(2,1)S(1)}, u32[]{:S(2)}, u32[]{:S(2)}) collective-permute-start(bf16[512,512]{1,0:T(8,128)(2,1)S(1)} %get-tuple-element.26.own_near), channel_id=1, source_target_pairs={{0,1},{1,0},{2,3},{3,2},{4,5},{5,4},{6,7},{7,6},{8,9},{9,8},{10,11... | collective-permute-start | bytes 1572872 | tf_op jit(solution)/shard_map/ppermute | solution.py:245
  24.4 17.1 %collective-permute-start.1 = (bf16[512,512]{1,0:T(8,128)(2,1)S(1)}, bf16[512,512]{1,0:T(8,128)(2,1)S(1)}, u32[]{:S(2)}, u32[]{:S(2)}) collective-permute-start(bf16[512,512]{1,0:T(8,128)(2,1)S(1)} %get-tuple-element.27.own_far), channel_id=1, source_target_pairs={{0,1},{1,0},{2,3},{3,2},{4,5},{5,4},{6,7},{7,6},{8,9},{9,8},{10,11... | collective-permute-start | bytes 1572872 | tf_op jit(solution)/shard_map/ppermute | solution.py:245
  34.7 13.7 %all-to-all-start.1 = ((bf16[16,32,128]{2,1,0:T(8,128)(2,1)}), bf16[16,32,128]{2,1,0:T(8,128)(2,1)S(1)}, u32[]{:S(2)}, u32[]{:S(2)}) async-start(bf16[16,32,128]{2,1,0:T(8,128)(2,1)} %get-tuple-element.25), calls=%async_computation.1 | async-start | bytes 262144 | tf_op jit(solution)/shard_map/all_to_all | solution.py:214
  137.8 19.2 %all-to-all-start.8 = ((f32[32,4,128]{2,1,0:T(4,128)}), f32[32,4,128]{2,1,0:T(4,128)S(1)}, u32[]{:S(2)}, u32[]{:S(2)}) async-start(f32[32,4,128]{2,1,0:T(4,128)} %shard_map.76), calls=%async_computation.8 | async-start | bytes 131072 | tf_op jit(solution)/shard_map/all_to_all | solution.py:214
  149.5 3.1 %collective-permute-start.2 = (f32[32,128]{1,0:T(8,128)S(1)}, f32[32,128]{1,0:T(8,128)S(1)}, u32[]{:S(2)}, u32[]{:S(2)}) collective-permute-start(f32[32,128]{1,0:T(8,128)S(1)} %get-tuple-element.38), channel_id=1, source_target_pairs={{0,1},{1,0},{2,3},{3,2},{4,5},{5,4},{6,7},{7,6},{8,9},{9,8},{10,11... | collective-permute-start | bytes 49160 | tf_op jit(solution)/shard_map/ppermute | solution.py:268

commit v6 on v5

--- a/solution.py
+++ b/solution.py
@@ -147,6 +147,17 @@
     sent_ref[...] = total.astype(BF)
 
 
+def own_kernel(front_ref, own_near, own_far, part_ref):
+    front = front_ref[...].astype(F32)
+    part_ref[...] = own_products(own_near, own_far, front, pltpu.roll(front, HALF, 1))
+
+
+def other_kernel(front_ref, part_ref, other_near, other_far, sent_ref):
+    front = front_ref[...].astype(F32)
+    total = part_ref[...] + other_products(other_near, other_far, front, pltpu.roll(front, HALF, 1))
+    sent_ref[...] = total.astype(BF)
+
+
 def found(level, parts_ref, hop_ref, kept_ref):
     arrived = parts_ref[0].astype(F32)
     for peer in range(1, parts_ref.shape[0]):
@@ -255,7 +266,11 @@
             kept,
         )
         front = exchanged(front, ROW).reshape(sources, ROOTS)
-        sent = call(level_kernel, bf(dests, ROOTS), [VMEM] * 5, front, *blocks)
+        if level == 1:
+            part = call(own_kernel, f32(dests, ROOTS), [VMEM] * 3, front, *blocks[:2])
+            sent = call(other_kernel, bf(dests, ROOTS), [VMEM] * 4, front, part, *blocks[2:])
+        else:
+            sent = call(level_kernel, bf(dests, ROOTS), [VMEM] * 5, front, *blocks)
     parts = exchanged(sent.reshape(z_all, PV, ROOTS), Z)
     mine, theirs, sums = call(
         last_kernel,

time: 158 us -> 158 us (level)
  blocking collectives: 94.7 us -> 108 us
  starting transfers between devices: 34.9 us -> 27.9 us
  waiting for transfers between devices: 19.6 us -> 12.8 us
    all_to_all x6 -> x7, blocking collectives: 86.2 us -> 99.6 us  [exchanged(): return lax.all_to_all(value, axis, 0, 0, tiled=True)]
    all_to_all x3 -> x2, starting transfers between devices: 28.1 us -> 21.1 us  [exchanged(): return lax.all_to_all(value, axis, 0, 0, tiled=True)]
    all_to_all x3 -> x2, waiting for transfers between devices: 18.8 us -> 12 us  [exchanged(): return lax.all_to_all(value, axis, 0, 0, tiled=True)]
    pallas_call x11 -> x12, Pallas kernels: 7.04 us -> 6.6 us  [call(): pl.pallas_call(kernel, out_shape=out_shape, in_specs=in_specs, out_specs=...]
  transfers between devices with their start and end apart: 6 -> 5, of which waited for: 4 -> 3; matrix products, arithmetic and copies ran while one was open for 0% -> 0% of each run, Pallas kernels for 0% -> 0%
where the time goes in v6:
time: 158 us; the launch traced here: 157 us
  blocking collectives  108 us (68%)
  starting transfers between devices  27.9 us (18%)
  waiting for transfers between devices  12.8 us (8%)
  Pallas kernels  6.6 us (4%)
    all_to_all x7, blocking collectives, exchanged(): return lax.all_to_all(value, axis, 0, 0, tiled=True)  99.6 us
    all_to_all x2, starting transfers between devices, exchanged(): return lax.all_to_all(value, axis, 0, 0, tiled=True)  21.1 us
    all_to_all x2, waiting for transfers between devices, exchanged(): return lax.all_to_all(value, axis, 0, 0, tiled=True)  12 us
    all_gather x1, blocking collectives, local(): both = lax.all_gather(theirs, C)  8.65 us
    pallas_call x12, Pallas kernels, call(): pl.pallas_call(kernel, out_shape=out_shape, in_specs=in_specs, out_specs=...  6.6 us
  transfers between devices with their start and end apart: 5, of which 3 were waited for; matrix products, arithmetic and copies ran while one was open for 0% of the time, Pallas kernels for 0%

profile of v6, /device:TPU:1, one launch (start us, length us, event | category | flops | bytes accessed | tf_op | source)
XLA Modules:
  0.0 156.9 jit_solution(18216240394817449919)
XLA Ops:
  1.3 1.8 %shard_map.67 = (bf16[512,512]{1,0:T(8,128)(2,1)S(1)}, bf16[512,512]{1,0:T(8,128)(2,1)S(1)}, bf16[512,128]{1,0:T(8,128)(2,1)S(1)}, bf16[512,128]{1,0:T(8,128)(2,...) custom-call(s32[1,1]{1,0:T(1,128)S(6)} %copy.7.total_ref, s32[2,32]{1,0:T(2,128)} %bitcast.20, ...), custom_call_target="tpu_custom_call" | custom-call | tf_op jit(solution)/shard_map/pallas_call | solution.py:29
  3.1 8.6 %all-gather = bf16[1024,128]{1,0:T(8,128)(2,1)S(1)} all-gather(bf16[512,128]{1,0:T(8,128)(2,1)S(1)} %get-tuple-element.22), channel_id=2, replica_groups=mesh['y'=4,'x'=4,'z'=16,'c'=2] {'c'}, dimensions={0}, use_global_device_ids=true | all-gather | bytes 393216 | tf_op jit(solution)/shard_map/all_gather | solution.py:255
  11.8 0.7 shard_map.68
  12.4 9.4 %all-to-all-start = ((bf16[16,32,128]{2,1,0:T(8,128)(2,1)}), bf16[16,32,128]{2,1,0:T(8,128)(2,1)S(1)}, u32[]{:S(2)}, u32[]{:S(2)}) async-start(bf16[16,32,128]{2,1,0:T(8,128)(2,1)} %bitcast.4), calls=%async_computation | async-start | bytes 262144 | tf_op jit(solution)/shard_map/all_to_all | solution.py:225
  21.8 2.6 %collective-permute-start = (bf16[512,512]{1,0:T(8,128)(2,1)S(1)}, bf16[512,512]{1,0:T(8,128)(2,1)S(1)}, u32[]{:S(2)}, u32[]{:S(2)}) collective-permute-start(bf16[512,512]{1,0:T(8,128)(2,1)S(1)} %get-tuple-element.26.own_near), channel_id=1, source_target_pairs={{0,1},{1,0},{2,3},{3,2},{4,5},{5,4},{6,7},{7,6},{8,9},{9,8},{10,11... | collective-permute-start | bytes 1572872 | tf_op jit(solution)/shard_map/ppermute | solution.py:256
  24.4 1.9 %collective-permute-start.1 = (bf16[512,512]{1,0:T(8,128)(2,1)S(1)}, bf16[512,512]{1,0:T(8,128)(2,1)S(1)}, u32[]{:S(2)}, u32[]{:S(2)}) collective-permute-start(bf16[512,512]{1,0:T(8,128)(2,1)S(1)} %get-tuple-element.27.own_far), channel_id=1, source_target_pairs={{0,1},{1,0},{2,3},{3,2},{4,5},{5,4},{6,7},{7,6},{8,9},{9,8},{10,11... | collective-permute-start | bytes 1572872 | tf_op jit(solution)/shard_map/ppermute | solution.py:256
  26.3 7.7 %all-to-all-done.parts_ref = bf16[16,32,128]{2,1,0:T(8,128)(2,1)S(1)} async-done(((bf16[16,32,128]{2,1,0:T(8,128)(2,1)}), bf16[16,32,128]{2,1,0:T(8,128)(2,1)S(1)}, u32[]{:S(2)}, u32[]{:S(2)}) %all-to-all-start) | async-done | bytes 131104 | tf_op jit(solution)/shard_map/all_to_all | solution.py:225
  34.0 13.4 %all_to_all.45 = bf16[16,32,128]{2,1,0:T(8,128)(2,1)S(1)} all-to-all(bf16[16,32,128]{2,1,0:T(8,128)(2,1)S(1)} %get-tuple-element.25), channel_id=1, replica_groups=mesh['y'=4,'x'=4,'z'=16,'c'=2] {'y','x'}, dimensions={0} | all-to-all | bytes 262144 | tf_op jit(solution)/shard_map/all_to_all | solution.py:225
  47.4 0.5 shard_map.70.part_ref
  47.9 0.0 collective-permute-done.other_near
  47.9 0.0 collective-permute-done.1.other_far
  47.9 0.5 shard_map.71
  48.4 18.2 %all_to_all.46.parts_ref = bf16[16,32,128]{2,1,0:T(8,128)(2,1)S(1)} all-to-all(bf16[16,32,128]{2,1,0:T(8,128)(2,1)S(1)} %bitcast.16), channel_id=1, replica_groups=mesh['y'=4,'x'=4,'z'=16,'c'=2] {'z'}, dimensions={0} | all-to-all | bytes 262144 | tf_op jit(solution)/shard_map/all_to_all | solution.py:225
  66.7 9.9 %all_to_all.47 = bf16[16,32,128]{2,1,0:T(8,128)(2,1)S(1)} all-to-all(bf16[16,32,128]{2,1,0:T(8,128)(2,1)S(1)} %get-tuple-element.30), channel_id=1, replica_groups=mesh['y'=4,'x'=4,'z'=16,'c'=2] {'y','x'}, dimensions={0} | all-to-all | bytes 262144 | tf_op jit(solution)/shard_map/all_to_all | solution.py:225
  76.7 0.8 shard_map.73
  77.4 16.9 %all_to_all.48.parts_ref = bf16[16,32,128]{2,1,0:T(8,128)(2,1)S(1)} all-to-all(bf16[16,32,128]{2,1,0:T(8,128)(2,1)S(1)} %bitcast.18), channel_id=1, replica_groups=mesh['y'=4,'x'=4,'z'=16,'c'=2] {'z'}, dimensions={0} | all-to-all | bytes 262144 | tf_op jit(solution)/shard_map/all_to_all | solution.py:225
  94.4 9.9 %all_to_all.49 = bf16[16,32,128]{2,1,0:T(8,128)(2,1)S(1)} all-to-all(bf16[16,32,128]{2,1,0:T(8,128)(2,1)S(1)} %get-tuple-element.33), channel_id=1, replica_groups=mesh['y'=4,'x'=4,'z'=16,'c'=2] {'y','x'}, dimensions={0} | all-to-all | bytes 262144 | tf_op jit(solution)/shard_map/all_to_all | solution.py:225
  104.3 0.8 shard_map.75
  105.1 15.8 %all_to_all.50.parts_ref = bf16[16,32,128]{2,1,0:T(8,128)(2,1)S(1)} all-to-all(bf16[16,32,128]{2,1,0:T(8,128)(2,1)S(1)} %bitcast.15), channel_id=1, replica_groups=mesh['y'=4,'x'=4,'z'=16,'c'=2] {'z'}, dimensions={0} | all-to-all | bytes 262144 | tf_op jit(solution)/shard_map/all_to_all | solution.py:225
  120.9 0.1 shard_map.76
  121.0 15.4 %all_to_all.51.parts_ref = f32[16,4,128]{2,1,0:T(4,128)S(1)} all-to-all(f32[16,4,128]{2,1,0:T(4,128)S(1)} %get-tuple-element.36), channel_id=1, replica_groups=mesh['y'=4,'x'=4,'z'=16,'c'=2] {'z'}, dimensions={0} | all-to-all | bytes 65536 | tf_op jit(solution)/shard_map/all_to_all | solution.py:225
  136.4 0.6 shard_map.77
  137.1 11.7 %all-to-all-start.8 = ((f32[32,4,128]{2,1,0:T(4,128)}), f32[32,4,128]{2,1,0:T(4,128)S(1)}, u32[]{:S(2)}, u32[]{:S(2)}) async-start(f32[32,4,128]{2,1,0:T(4,128)} %shard_map.77), calls=%async_computation.8 | async-start | bytes 131072 | tf_op jit(solution)/shard_map/all_to_all | solution.py:225
  148.8 2.3 %collective-permute-start.2 = (f32[32,128]{1,0:T(8,128)S(1)}, f32[32,128]{1,0:T(8,128)S(1)}, u32[]{:S(2)}, u32[]{:S(2)}) collective-permute-start(f32[32,128]{1,0:T(8,128)S(1)} %get-tuple-element.38), channel_id=1, source_target_pairs={{0,1},{1,0},{2,3},{3,2},{4,5},{5,4},{6,7},{7,6},{8,9},{9,8},{10,11... | collective-permute-start | bytes 49160 | tf_op jit(solution)/shard_map/ppermute | solution.py:283
  151.1 0.8 collective-permute-done.2.theirs_ref
  151.9 4.4 %all-to-all-done.8.sums_ref = f32[32,4,128]{2,1,0:T(4,128)S(1)} async-done(((f32[32,4,128]{2,1,0:T(4,128)}), f32[32,4,128]{2,1,0:T(4,128)S(1)}, u32[]{:S(2)}, u32[]{:S(2)}) %all-to-all-start.8) | async-done | bytes 65568 | tf_op jit(solution)/shard_map/all_to_all | solution.py:225
  156.2 0.7 shard_map.78
  (3 shorter events, 0.1 us)
Async XLA Ops:
  12.4 21.6 %all-to-all-start = ((bf16[16,32,128]{2,1,0:T(8,128)(2,1)}), bf16[16,32,128]{2,1,0:T(8,128)(2,1)S(1)}, u32[]{:S(2)}, u32[]{:S(2)}) async-start(bf16[16,32,128]{2,1,0:T(8,128)(2,1)} %bitcast.4), calls=%async_computation | async-start | bytes 262144 | tf_op jit(solution)/shard_map/all_to_all | solution.py:225
  21.8 26.1 %collective-permute-start = (bf16[512,512]{1,0:T(8,128)(2,1)S(1)}, bf16[512,512]{1,0:T(8,128)(2,1)S(1)}, u32[]{:S(2)}, u32[]{:S(2)}) collective-permute-start(bf16[512,512]{1,0:T(8,128)(2,1)S(1)} %get-tuple-element.26.own_near), channel_id=1, source_target_pairs={{0,1},{1,0},{2,3},{3,2},{4,5},{5,4},{6,7},{7,6},{8,9},{9,8},{10,11... | collective-permute-start | bytes 1572872 | tf_op jit(solution)/shard_map/ppermute | solution.py:256
  24.4 23.5 %collective-permute-start.1 = (bf16[512,512]{1,0:T(8,128)(2,1)S(1)}, bf16[512,512]{1,0:T(8,128)(2,1)S(1)}, u32[]{:S(2)}, u32[]{:S(2)}) collective-permute-start(bf16[512,512]{1,0:T(8,128)(2,1)S(1)} %get-tuple-element.27.own_far), channel_id=1, source_target_pairs={{0,1},{1,0},{2,3},{3,2},{4,5},{5,4},{6,7},{7,6},{8,9},{9,8},{10,11... | collective-permute-start | bytes 1572872 | tf_op jit(solution)/shard_map/ppermute | solution.py:256
  137.1 19.2 %all-to-all-start.8 = ((f32[32,4,128]{2,1,0:T(4,128)}), f32[32,4,128]{2,1,0:T(4,128)S(1)}, u32[]{:S(2)}, u32[]{:S(2)}) async-start(f32[32,4,128]{2,1,0:T(4,128)} %shard_map.77), calls=%async_computation.8 | async-start | bytes 131072 | tf_op jit(solution)/shard_map/all_to_all | solution.py:225
  148.8 3.1 %collective-permute-start.2 = (f32[32,128]{1,0:T(8,128)S(1)}, f32[32,128]{1,0:T(8,128)S(1)}, u32[]{:S(2)}, u32[]{:S(2)}) collective-permute-start(f32[32,128]{1,0:T(8,128)S(1)} %get-tuple-element.38), channel_id=1, source_target_pairs={{0,1},{1,0},{2,3},{3,2},{4,5},{5,4},{6,7},{7,6},{8,9},{9,8},{10,11... | collective-permute-start | bytes 49160 | tf_op jit(solution)/shard_map/ppermute | solution.py:283

commit v7 on v6

--- a/solution.py
+++ b/solution.py
@@ -51,6 +51,7 @@
     pos_ref,
     tiles_ref,
     roots_ref,
+    values_ref,
     pos_sem,
     roots_sem,
     tile_sems,
@@ -80,13 +81,14 @@
                 block_ref[pl.ds(rows, PV), pl.ds(lanes, TILE)] = tiles_ref[slot, pl.ds(first, PV), :]
         return carry
 
+    roots_copy.wait()
+    first_values(row_block, roots_ref, values_ref, hop_ref, kept_ref)
     pos_copy.wait()
     for chunk in range(CHUNKS):
         tile_copies[chunk].wait()
         lax.fori_loop(chunk * step, jnp.minimum(total_ref[0, 0], (chunk + 1) * step), place, 0)
 
-    roots_copy.wait()
-    first_products(row_block, roots_ref, near_ref, far_ref, mine_ref, theirs_ref, hop_ref, kept_ref)
+    first_products(values_ref, near_ref, far_ref, mine_ref, theirs_ref)
 
 
 def left_half(shape):
@@ -114,25 +116,28 @@
     return times(near_ref, jnp.where(left, zero, front)) + times(far_ref, jnp.where(left, turned, zero))
 
 
-def first_products(row_block, roots_ref, near_ref, far_ref, mine_ref, theirs_ref, hop_ref, kept_ref):
+def first_values(row_block, roots_ref, values_ref, hop_ref, kept_ref):
     core, pair = lax.axis_index(C), lax.axis_index(Z) * 2 * PV
     base_own, base_other = pair + core * PV, pair + (1 - core) * PV
     roots = own_roots(roots_ref)
     turned = pltpu.roll(roots, HALF, 1)
-    shape = (near_ref.shape[1], ROOTS)
-    row = lax.broadcasted_iota(jnp.int32, shape, 0)
+    row = lax.broadcasted_iota(jnp.int32, values_ref.shape[1:], 0)
     vertex = (row // PV) * row_block + row % PV + base_own
-    near = times(near_ref, (vertex == roots).astype(F32))
-    far = times(far_ref, (vertex == turned).astype(F32))
-    left = left_half(near.shape)
-    mine_ref[...] = jnp.where(left, near, far).astype(BF)
-    theirs_ref[...] = jnp.where(left, far, near).astype(BF)
+    values_ref[0] = (vertex == roots).astype(F32).astype(BF)
+    values_ref[1] = (vertex == turned).astype(F32).astype(BF)
     state = hop_ref.shape
     left = left_half(state)
     vertex = lax.broadcasted_iota(jnp.int32, state, 0) + lax.axis_index(ROW) * row_block
     is_root = vertex + jnp.where(left, base_own, base_other) == jnp.where(left, roots, turned)
     kept_ref[...] = is_root.astype(F32)
     hop_ref[...] = jnp.where(is_root, 0, LEVELS + 1)
+
+
+def first_products(values_ref, near_ref, far_ref, mine_ref, theirs_ref):
+    near, far = times(near_ref, values_ref[0]), times(far_ref, values_ref[1])
+    left = left_half(near.shape)
+    mine_ref[...] = jnp.where(left, near, far).astype(BF)
+    theirs_ref[...] = jnp.where(left, far, near).astype(BF)
 
 
 def add_kernel(mine_ref, both_ref, sent_ref):
@@ -247,6 +252,7 @@
             pltpu.SMEM((2, slots), jnp.int32),
             pltpu.VMEM((slots, TILE, TILE), BF),
             pltpu.VMEM((1, ROOTS), jnp.int32),
+            pltpu.VMEM((2, sources, ROOTS), BF),
             pltpu.SemaphoreType.DMA,
             pltpu.SemaphoreType.DMA,
             pltpu.SemaphoreType.DMA((CHUNKS,)),
@@ -281,7 +287,7 @@
         kept,
     )
     theirs = lax.ppermute(theirs, C, swap)
-    sums = exchanged(sums, Z)
+    sums, theirs = lax.optimization_barrier((exchanged(sums, Z), theirs))
     sums = call(sum_kernel, f32(2 * rows_all, LEVELS, ROOTS), [VMEM], sums)
     sums = exchanged(sums, (Y, X, C))
     return call(end_kernel, (hops, f32(PV, ROOTS), f32(LEVELS, ROOTS)), [VMEM] * 3, sums, mine, theirs)

time: 158 us -> 157 us (level)
  blocking collectives: 108 us -> 112 us
  waiting for transfers between devices: 12.8 us -> 10.1 us
    all_to_all x2, starting transfers between devices: 21.1 us -> 13.3 us  [exchanged(): return lax.all_to_all(value, axis, 0, 0, tiled=True)]
    ppermute x1, starting transfers between devices: 2.26 us -> 9.12 us  [local(): theirs = lax.ppermute(theirs, C, swap)]
    all_to_all x7, blocking collectives: 99.6 us -> 103 us  [exchanged(): return lax.all_to_all(value, axis, 0, 0, tiled=True)]
    all_to_all x2, waiting for transfers between devices: 12 us -> 9.29 us  [exchanged(): return lax.all_to_all(value, axis, 0, 0, tiled=True)]
where the time goes in v7:
time: 157 us
  blocking collectives  112 us (71%)
  starting transfers between devices  26.8 us (17%)
  waiting for transfers between devices  10.1 us (6%)
  Pallas kernels  6.65 us (4%)
    all_to_all x7, blocking collectives, exchanged(): return lax.all_to_all(value, axis, 0, 0, tiled=True)  103 us
    all_to_all x2, starting transfers between devices, exchanged(): return lax.all_to_all(value, axis, 0, 0, tiled=True)  13.3 us
    all_to_all x2, waiting for transfers between devices, exchanged(): return lax.all_to_all(value, axis, 0, 0, tiled=True)  9.29 us
    ppermute x1, starting transfers between devices, local(): theirs = lax.ppermute(theirs, C, swap)  9.12 us
    all_gather x1, blocking collectives, local(): both = lax.all_gather(theirs, C)  8.65 us
    pallas_call x12, Pallas kernels, call(): pl.pallas_call(kernel, out_shape=out_shape, in_specs=in_specs, out_specs=...  6.65 us
  transfers between devices with their start and end apart: 5, of which 3 were waited for; matrix products, arithmetic and copies ran while one was open for 0% of the time, Pallas kernels for 0%

profile of v7, /device:TPU:1, one launch (start us, length us, event | category | flops | bytes accessed | tf_op | source)
XLA Modules:
  0.0 156.7 jit_solution(16455244202261261014)
XLA Ops:
  1.3 1.9 %shard_map.67 = (bf16[512,512]{1,0:T(8,128)(2,1)S(1)}, bf16[512,512]{1,0:T(8,128)(2,1)S(1)}, bf16[512,128]{1,0:T(8,128)(2,1)S(1)}, bf16[512,128]{1,0:T(8,128)(2,...) custom-call(s32[1,1]{1,0:T(1,128)S(6)} %copy.7.total_ref, s32[2,32]{1,0:T(2,128)} %bitcast.20, ...), custom_call_target="tpu_custom_call" | custom-call | tf_op jit(solution)/shard_map/pallas_call | solution.py:29
  3.2 8.6 %all-gather = bf16[1024,128]{1,0:T(8,128)(2,1)S(1)} all-gather(bf16[512,128]{1,0:T(8,128)(2,1)S(1)} %get-tuple-element.24), channel_id=2, replica_groups=mesh['y'=4,'x'=4,'z'=16,'c'=2] {'c'}, dimensions={0}, use_global_device_ids=true | all-gather | bytes 393216 | tf_op jit(solution)/shard_map/all_gather | solution.py:261
  11.8 0.7 shard_map.68
  12.5 9.2 %all-to-all-start = ((bf16[16,32,128]{2,1,0:T(8,128)(2,1)}), bf16[16,32,128]{2,1,0:T(8,128)(2,1)S(1)}, u32[]{:S(2)}, u32[]{:S(2)}) async-start(bf16[16,32,128]{2,1,0:T(8,128)(2,1)} %bitcast.4), calls=%async_computation | async-start | bytes 262144 | tf_op jit(solution)/shard_map/all_to_all | solution.py:230
  21.7 2.5 %collective-permute-start = (bf16[512,512]{1,0:T(8,128)(2,1)S(1)}, bf16[512,512]{1,0:T(8,128)(2,1)S(1)}, u32[]{:S(2)}, u32[]{:S(2)}) collective-permute-start(bf16[512,512]{1,0:T(8,128)(2,1)S(1)} %get-tuple-element.28.own_near), channel_id=1, source_target_pairs={{0,1},{1,0},{2,3},{3,2},{4,5},{5,4},{6,7},{7,6},{8,9},{9,8},{10,11... | collective-permute-start | bytes 1572872 | tf_op jit(solution)/shard_map/ppermute | solution.py:262
  24.3 1.9 %collective-permute-start.1 = (bf16[512,512]{1,0:T(8,128)(2,1)S(1)}, bf16[512,512]{1,0:T(8,128)(2,1)S(1)}, u32[]{:S(2)}, u32[]{:S(2)}) collective-permute-start(bf16[512,512]{1,0:T(8,128)(2,1)S(1)} %get-tuple-element.29.own_far), channel_id=1, source_target_pairs={{0,1},{1,0},{2,3},{3,2},{4,5},{5,4},{6,7},{7,6},{8,9},{9,8},{10,11... | collective-permute-start | bytes 1572872 | tf_op jit(solution)/shard_map/ppermute | solution.py:262
  26.2 7.7 %all-to-all-done.parts_ref = bf16[16,32,128]{2,1,0:T(8,128)(2,1)S(1)} async-done(((bf16[16,32,128]{2,1,0:T(8,128)(2,1)}), bf16[16,32,128]{2,1,0:T(8,128)(2,1)S(1)}, u32[]{:S(2)}, u32[]{:S(2)}) %all-to-all-start) | async-done | bytes 131104 | tf_op jit(solution)/shard_map/all_to_all | solution.py:230
  33.9 13.5 %all_to_all.45 = bf16[16,32,128]{2,1,0:T(8,128)(2,1)S(1)} all-to-all(bf16[16,32,128]{2,1,0:T(8,128)(2,1)S(1)} %get-tuple-element.27), channel_id=1, replica_groups=mesh['y'=4,'x'=4,'z'=16,'c'=2] {'y','x'}, dimensions={0} | all-to-all | bytes 262144 | tf_op jit(solution)/shard_map/all_to_all | solution.py:230
  47.4 0.5 shard_map.70.part_ref
  47.9 0.0 collective-permute-done.other_near
  47.9 0.0 collective-permute-done.1.other_far
  48.0 0.5 shard_map.71
  48.5 18.2 %all_to_all.46.parts_ref = bf16[16,32,128]{2,1,0:T(8,128)(2,1)S(1)} all-to-all(bf16[16,32,128]{2,1,0:T(8,128)(2,1)S(1)} %bitcast.16), channel_id=1, replica_groups=mesh['y'=4,'x'=4,'z'=16,'c'=2] {'z'}, dimensions={0} | all-to-all | bytes 262144 | tf_op jit(solution)/shard_map/all_to_all | solution.py:230
  66.7 9.9 %all_to_all.47 = bf16[16,32,128]{2,1,0:T(8,128)(2,1)S(1)} all-to-all(bf16[16,32,128]{2,1,0:T(8,128)(2,1)S(1)} %get-tuple-element.32), channel_id=1, replica_groups=mesh['y'=4,'x'=4,'z'=16,'c'=2] {'y','x'}, dimensions={0} | all-to-all | bytes 262144 | tf_op jit(solution)/shard_map/all_to_all | solution.py:230
  76.7 0.8 shard_map.73
  77.5 16.9 %all_to_all.48.parts_ref = bf16[16,32,128]{2,1,0:T(8,128)(2,1)S(1)} all-to-all(bf16[16,32,128]{2,1,0:T(8,128)(2,1)S(1)} %bitcast.18), channel_id=1, replica_groups=mesh['y'=4,'x'=4,'z'=16,'c'=2] {'z'}, dimensions={0} | all-to-all | bytes 262144 | tf_op jit(solution)/shard_map/all_to_all | solution.py:230
  94.4 9.9 %all_to_all.49 = bf16[16,32,128]{2,1,0:T(8,128)(2,1)S(1)} all-to-all(bf16[16,32,128]{2,1,0:T(8,128)(2,1)S(1)} %get-tuple-element.35), channel_id=1, replica_groups=mesh['y'=4,'x'=4,'z'=16,'c'=2] {'y','x'}, dimensions={0} | all-to-all | bytes 262144 | tf_op jit(solution)/shard_map/all_to_all | solution.py:230
  104.3 0.8 shard_map.75
  105.1 15.8 %all_to_all.50.parts_ref = bf16[16,32,128]{2,1,0:T(8,128)(2,1)S(1)} all-to-all(bf16[16,32,128]{2,1,0:T(8,128)(2,1)S(1)} %bitcast.15), channel_id=1, replica_groups=mesh['y'=4,'x'=4,'z'=16,'c'=2] {'z'}, dimensions={0} | all-to-all | bytes 262144 | tf_op jit(solution)/shard_map/all_to_all | solution.py:230
  120.9 0.7 shard_map.76
  121.6 4.0 %all-to-all-start.7 = ((f32[16,4,128]{2,1,0:T(4,128)}), f32[16,4,128]{2,1,0:T(4,128)S(1)}, u32[]{:S(2)}, u32[]{:S(2)}) async-start(f32[16,4,128]{2,1,0:T(4,128)} %get-tuple-element.38), calls=%async_computation.7 | async-start | bytes 65536 | tf_op jit(solution)/shard_map/all_to_all | solution.py:230
  125.7 9.1 %collective-permute-start.2 = (f32[32,128]{1,0:T(8,128)S(1)}, f32[32,128]{1,0:T(8,128)S(1)}, u32[]{:S(2)}, u32[]{:S(2)}) collective-permute-start(f32[32,128]{1,0:T(8,128)S(1)} %get-tuple-element.39), channel_id=1, source_target_pairs={{0,1},{1,0},{2,3},{3,2},{4,5},{5,4},{6,7},{7,6},{8,9},{9,8},{10,11... | collective-permute-start | bytes 49160 | tf_op jit(solution)/shard_map/ppermute | solution.py:289
  134.8 0.8 collective-permute-done.2.theirs_ref
  135.6 1.6 %all-to-all-done.7.parts_ref = f32[16,4,128]{2,1,0:T(4,128)S(1)} async-done(((f32[16,4,128]{2,1,0:T(4,128)}), f32[16,4,128]{2,1,0:T(4,128)S(1)}, u32[]{:S(2)}, u32[]{:S(2)}) %all-to-all-start.7) | async-done | bytes 32800 | tf_op jit(solution)/shard_map/all_to_all | solution.py:230
  137.3 18.7 %all_to_all.51.sums_ref = f32[32,4,128]{2,1,0:T(4,128)S(1)} all-to-all(f32[32,4,128]{2,1,0:T(4,128)S(1)} %shard_map.77), channel_id=1, replica_groups=mesh['y'=4,'x'=4,'z'=16,'c'=2] {'y','x','c'}, dimensions={0} | all-to-all | bytes 131072 | tf_op jit(solution)/shard_map/all_to_all | solution.py:230
  156.0 0.7 shard_map.78
  (4 shorter events, 0.1 us)
Async XLA Ops:
  12.5 21.4 %all-to-all-start = ((bf16[16,32,128]{2,1,0:T(8,128)(2,1)}), bf16[16,32,128]{2,1,0:T(8,128)(2,1)S(1)}, u32[]{:S(2)}, u32[]{:S(2)}) async-start(bf16[16,32,128]{2,1,0:T(8,128)(2,1)} %bitcast.4), calls=%async_computation | async-start | bytes 262144 | tf_op jit(solution)/shard_map/all_to_all | solution.py:230
  21.7 26.2 %collective-permute-start = (bf16[512,512]{1,0:T(8,128)(2,1)S(1)}, bf16[512,512]{1,0:T(8,128)(2,1)S(1)}, u32[]{:S(2)}, u32[]{:S(2)}) collective-permute-start(bf16[512,512]{1,0:T(8,128)(2,1)S(1)} %get-tuple-element.28.own_near), channel_id=1, source_target_pairs={{0,1},{1,0},{2,3},{3,2},{4,5},{5,4},{6,7},{7,6},{8,9},{9,8},{10,11... | collective-permute-start | bytes 1572872 | tf_op jit(solution)/shard_map/ppermute | solution.py:262
  24.3 23.7 %collective-permute-start.1 = (bf16[512,512]{1,0:T(8,128)(2,1)S(1)}, bf16[512,512]{1,0:T(8,128)(2,1)S(1)}, u32[]{:S(2)}, u32[]{:S(2)}) collective-permute-start(bf16[512,512]{1,0:T(8,128)(2,1)S(1)} %get-tuple-element.29.own_far), channel_id=1, source_target_pairs={{0,1},{1,0},{2,3},{3,2},{4,5},{5,4},{6,7},{7,6},{8,9},{9,8},{10,11... | collective-permute-start | bytes 1572872 | tf_op jit(solution)/shard_map/ppermute | solution.py:262
  121.6 15.6 %all-to-all-start.7 = ((f32[16,4,128]{2,1,0:T(4,128)}), f32[16,4,128]{2,1,0:T(4,128)S(1)}, u32[]{:S(2)}, u32[]{:S(2)}) async-start(f32[16,4,128]{2,1,0:T(4,128)} %get-tuple-element.38), calls=%async_computation.7 | async-start | bytes 65536 | tf_op jit(solution)/shard_map/all_to_all | solution.py:230
  125.7 9.9 %collective-permute-start.2 = (f32[32,128]{1,0:T(8,128)S(1)}, f32[32,128]{1,0:T(8,128)S(1)}, u32[]{:S(2)}, u32[]{:S(2)}) collective-permute-start(f32[32,128]{1,0:T(8,128)S(1)} %get-tuple-element.39), channel_id=1, source_target_pairs={{0,1},{1,0},{2,3},{3,2},{4,5},{5,4},{6,7},{7,6},{8,9},{9,8},{10,11... | collective-permute-start | bytes 49160 | tf_op jit(solution)/shard_map/ppermute | solution.py:289

commit v8 on v7

--- a/solution.py
+++ b/solution.py
@@ -67,26 +67,29 @@
     for chunk in range(CHUNKS):
         part = pl.ds(chunk * step, step)
         tile_copies.append(pltpu.make_async_copy(tiles_hbm.at[part], tiles_ref.at[part], tile_sems.at[chunk]))
-        tile_copies[-1].start()
+    for copy in reversed(tile_copies):
+        copy.start()
     for block_ref in (near_ref, far_ref):
         block_ref[...] = jnp.zeros_like(block_ref)
-
-    def place(slot, carry):
-        dest, source = pos_ref[0, slot], pos_ref[1, slot]
-        for part in range(2):
-            for half, block_ref in enumerate((near_ref, far_ref)):
-                first = pl.multiple_of(part * 2 * PV + (half ^ core) * PV, PV)
-                rows = pl.multiple_of(dest * 2 * PV + part * PV, PV)
-                lanes = pl.multiple_of(source * TILE, TILE)
-                block_ref[pl.ds(rows, PV), pl.ds(lanes, TILE)] = tiles_ref[slot, pl.ds(first, PV), :]
-        return carry
 
     roots_copy.wait()
     first_values(row_block, roots_ref, values_ref, hop_ref, kept_ref)
     pos_copy.wait()
-    for chunk in range(CHUNKS):
+    total = total_ref[0, 0]
+    row_tiles, column_tiles = near_ref.shape[0] // (2 * PV), near_ref.shape[1] // TILE
+    for chunk in reversed(range(CHUNKS)):
         tile_copies[chunk].wait()
-        lax.fori_loop(chunk * step, jnp.minimum(total_ref[0, 0], (chunk + 1) * step), place, 0)
+        for slot in reversed(range(chunk * step, (chunk + 1) * step)):
+            dest = jnp.minimum(pos_ref[0, slot], row_tiles - 1)
+            source = jnp.minimum(pos_ref[1, slot], column_tiles - 1)
+            lanes = pl.ds(pl.multiple_of(source * TILE, TILE), TILE)
+            used = slot < total
+            for part in range(2):
+                for half, block_ref in enumerate((near_ref, far_ref)):
+                    first = pl.multiple_of(part * 2 * PV + (half ^ core) * PV, PV)
+                    rows = pl.multiple_of(dest * 2 * PV + part * PV, PV)
+                    tile = tiles_ref[slot, pl.ds(first, PV), :]
+                    block_ref[pl.ds(rows, PV), lanes] = jnp.where(used, tile, jnp.zeros_like(tile))
 
     first_products(values_ref, near_ref, far_ref, mine_ref, theirs_ref)
 
@@ -152,14 +155,14 @@
     sent_ref[...] = total.astype(BF)
 
 
-def own_kernel(front_ref, own_near, own_far, part_ref):
-    front = front_ref[...].astype(F32)
-    part_ref[...] = own_products(own_near, own_far, front, pltpu.roll(front, HALF, 1))
-
-
-def other_kernel(front_ref, part_ref, other_near, other_far, sent_ref):
-    front = front_ref[...].astype(F32)
-    total = part_ref[...] + other_products(other_near, other_far, front, pltpu.roll(front, HALF, 1))
+def turn_kernel(front_ref, turned_ref):
+    turned_ref[...] = pltpu.roll(front_ref[...].astype(F32), HALF, 1).astype(BF)
+
+
+def turned_kernel(front_ref, turned_ref, own_near, own_far, other_near, other_far, sent_ref):
+    front, turned = front_ref[...].astype(F32), turned_ref[...].astype(F32)
+    total = own_products(own_near, own_far, front, turned)
+    total += other_products(other_near, other_far, front, turned)
     sent_ref[...] = total.astype(BF)
 
 
@@ -273,8 +276,8 @@
         )
         front = exchanged(front, ROW).reshape(sources, ROOTS)
         if level == 1:
-            part = call(own_kernel, f32(dests, ROOTS), [VMEM] * 3, front, *blocks[:2])
-            sent = call(other_kernel, bf(dests, ROOTS), [VMEM] * 4, front, part, *blocks[2:])
+            turned = call(turn_kernel, bf(sources, ROOTS), [VMEM], front)
+            sent = call(turned_kernel, bf(dests, ROOTS), [VMEM] * 6, front, turned, *blocks)
         else:
             sent = call(level_kernel, bf(dests, ROOTS), [VMEM] * 5, front, *blocks)
     parts = exchanged(sent.reshape(z_all, PV, ROOTS), Z)

time: 157 us -> 157 us (level)
  no operation moved by 1% of the time
where the time goes in v8:
time: 157 us; the launch traced here: 156 us
  blocking collectives  111 us (71%)
  starting transfers between devices  27.2 us (17%)
  waiting for transfers between devices  10.1 us (6%)
  Pallas kernels  6.42 us (4%)
    all_to_all x7, blocking collectives, exchanged(): return lax.all_to_all(value, axis, 0, 0, tiled=True)  103 us
    all_to_all x2, starting transfers between devices, exchanged(): return lax.all_to_all(value, axis, 0, 0, tiled=True)  13.6 us
    all_to_all x2, waiting for transfers between devices, exchanged(): return lax.all_to_all(value, axis, 0, 0, tiled=True)  9.29 us
    ppermute x1, starting transfers between devices, local(): theirs = lax.ppermute(theirs, C, swap)  9.12 us
    all_gather x1, blocking collectives, local(): both = lax.all_gather(theirs, C)  8.51 us
    pallas_call x12, Pallas kernels, call(): pl.pallas_call(kernel, out_shape=out_shape, in_specs=in_specs, out_specs=...  6.42 us
  transfers between devices with their start and end apart: 5, of which 3 were waited for; matrix products, arithmetic and copies ran while one was open for 0% of the time, Pallas kernels for 0%

profile of v8, /device:TPU:1, one launch (start us, length us, event | category | flops | bytes accessed | tf_op | source)
XLA Modules:
  0.0 156.5 jit_solution(7762244373025729137)
XLA Ops:
  1.3 1.8 %shard_map.67 = (bf16[512,512]{1,0:T(8,128)(2,1)S(1)}, bf16[512,512]{1,0:T(8,128)(2,1)S(1)}, bf16[512,128]{1,0:T(8,128)(2,1)S(1)}, bf16[512,128]{1,0:T(8,128)(2,...) custom-call(s32[1,1]{1,0:T(1,128)S(6)} %copy.7.total_ref, s32[2,32]{1,0:T(2,128)} %bitcast.20, ...), custom_call_target="tpu_custom_call" | custom-call | tf_op jit(solution)/shard_map/pallas_call | solution.py:29
  3.1 8.5 %all-gather = bf16[1024,128]{1,0:T(8,128)(2,1)S(1)} all-gather(bf16[512,128]{1,0:T(8,128)(2,1)S(1)} %get-tuple-element.24), channel_id=2, replica_groups=mesh['y'=4,'x'=4,'z'=16,'c'=2] {'c'}, dimensions={0}, use_global_device_ids=true | all-gather | bytes 393216 | tf_op jit(solution)/shard_map/all_gather | solution.py:264
  11.6 0.7 shard_map.68
  12.3 9.5 %all-to-all-start = ((bf16[16,32,128]{2,1,0:T(8,128)(2,1)}), bf16[16,32,128]{2,1,0:T(8,128)(2,1)S(1)}, u32[]{:S(2)}, u32[]{:S(2)}) async-start(bf16[16,32,128]{2,1,0:T(8,128)(2,1)} %bitcast.4), calls=%async_computation | async-start | bytes 262144 | tf_op jit(solution)/shard_map/all_to_all | solution.py:233
  21.9 2.6 %collective-permute-start = (bf16[512,512]{1,0:T(8,128)(2,1)S(1)}, bf16[512,512]{1,0:T(8,128)(2,1)S(1)}, u32[]{:S(2)}, u32[]{:S(2)}) collective-permute-start(bf16[512,512]{1,0:T(8,128)(2,1)S(1)} %get-tuple-element.28.own_near), channel_id=1, source_target_pairs={{0,1},{1,0},{2,3},{3,2},{4,5},{5,4},{6,7},{7,6},{8,9},{9,8},{10,11... | collective-permute-start | bytes 1572872 | tf_op jit(solution)/shard_map/ppermute | solution.py:265
  24.4 1.9 %collective-permute-start.1 = (bf16[512,512]{1,0:T(8,128)(2,1)S(1)}, bf16[512,512]{1,0:T(8,128)(2,1)S(1)}, u32[]{:S(2)}, u32[]{:S(2)}) collective-permute-start(bf16[512,512]{1,0:T(8,128)(2,1)S(1)} %get-tuple-element.29.own_far), channel_id=1, source_target_pairs={{0,1},{1,0},{2,3},{3,2},{4,5},{5,4},{6,7},{7,6},{8,9},{9,8},{10,11... | collective-permute-start | bytes 1572872 | tf_op jit(solution)/shard_map/ppermute | solution.py:265
  26.3 7.7 %all-to-all-done.parts_ref = bf16[16,32,128]{2,1,0:T(8,128)(2,1)S(1)} async-done(((bf16[16,32,128]{2,1,0:T(8,128)(2,1)}), bf16[16,32,128]{2,1,0:T(8,128)(2,1)S(1)}, u32[]{:S(2)}, u32[]{:S(2)}) %all-to-all-start) | async-done | bytes 131104 | tf_op jit(solution)/shard_map/all_to_all | solution.py:233
  34.0 13.4 %all_to_all.45 = bf16[16,32,128]{2,1,0:T(8,128)(2,1)S(1)} all-to-all(bf16[16,32,128]{2,1,0:T(8,128)(2,1)S(1)} %get-tuple-element.27), channel_id=1, replica_groups=mesh['y'=4,'x'=4,'z'=16,'c'=2] {'y','x'}, dimensions={0} | all-to-all | bytes 262144 | tf_op jit(solution)/shard_map/all_to_all | solution.py:233
  47.4 0.1 shard_map.70.turned_ref
  47.5 0.0 collective-permute-done.other_near
  47.5 0.0 collective-permute-done.1.other_far
  47.6 0.7 shard_map.71
  48.3 18.2 %all_to_all.46.parts_ref = bf16[16,32,128]{2,1,0:T(8,128)(2,1)S(1)} all-to-all(bf16[16,32,128]{2,1,0:T(8,128)(2,1)S(1)} %bitcast.16), channel_id=1, replica_groups=mesh['y'=4,'x'=4,'z'=16,'c'=2] {'z'}, dimensions={0} | all-to-all | bytes 262144 | tf_op jit(solution)/shard_map/all_to_all | solution.py:233
  66.5 9.9 %all_to_all.47 = bf16[16,32,128]{2,1,0:T(8,128)(2,1)S(1)} all-to-all(bf16[16,32,128]{2,1,0:T(8,128)(2,1)S(1)} %get-tuple-element.32), channel_id=1, replica_groups=mesh['y'=4,'x'=4,'z'=16,'c'=2] {'y','x'}, dimensions={0} | all-to-all | bytes 262144 | tf_op jit(solution)/shard_map/all_to_all | solution.py:233
  76.5 0.8 shard_map.73
  77.3 16.9 %all_to_all.48.parts_ref = bf16[16,32,128]{2,1,0:T(8,128)(2,1)S(1)} all-to-all(bf16[16,32,128]{2,1,0:T(8,128)(2,1)S(1)} %bitcast.18), channel_id=1, replica_groups=mesh['y'=4,'x'=4,'z'=16,'c'=2] {'z'}, dimensions={0} | all-to-all | bytes 262144 | tf_op jit(solution)/shard_map/all_to_all | solution.py:233
  94.2 9.9 %all_to_all.49 = bf16[16,32,128]{2,1,0:T(8,128)(2,1)S(1)} all-to-all(bf16[16,32,128]{2,1,0:T(8,128)(2,1)S(1)} %get-tuple-element.35), channel_id=1, replica_groups=mesh['y'=4,'x'=4,'z'=16,'c'=2] {'y','x'}, dimensions={0} | all-to-all | bytes 262144 | tf_op jit(solution)/shard_map/all_to_all | solution.py:233
  104.1 0.8 shard_map.75
  104.9 15.8 %all_to_all.50.parts_ref = bf16[16,32,128]{2,1,0:T(8,128)(2,1)S(1)} all-to-all(bf16[16,32,128]{2,1,0:T(8,128)(2,1)S(1)} %bitcast.15), channel_id=1, replica_groups=mesh['y'=4,'x'=4,'z'=16,'c'=2] {'z'}, dimensions={0} | all-to-all | bytes 262144 | tf_op jit(solution)/shard_map/all_to_all | solution.py:233
  120.7 0.7 shard_map.76
  121.4 4.0 %all-to-all-start.7 = ((f32[16,4,128]{2,1,0:T(4,128)}), f32[16,4,128]{2,1,0:T(4,128)S(1)}, u32[]{:S(2)}, u32[]{:S(2)}) async-start(f32[16,4,128]{2,1,0:T(4,128)} %get-tuple-element.38), calls=%async_computation.7 | async-start | bytes 65536 | tf_op jit(solution)/shard_map/all_to_all | solution.py:233
  125.5 9.1 %collective-permute-start.2 = (f32[32,128]{1,0:T(8,128)S(1)}, f32[32,128]{1,0:T(8,128)S(1)}, u32[]{:S(2)}, u32[]{:S(2)}) collective-permute-start(f32[32,128]{1,0:T(8,128)S(1)} %get-tuple-element.39), channel_id=1, source_target_pairs={{0,1},{1,0},{2,3},{3,2},{4,5},{5,4},{6,7},{7,6},{8,9},{9,8},{10,11... | collective-permute-start | bytes 49160 | tf_op jit(solution)/shard_map/ppermute | solution.py:292
  134.6 0.8 collective-permute-done.2.theirs_ref
  135.4 1.6 %all-to-all-done.7.parts_ref = f32[16,4,128]{2,1,0:T(4,128)S(1)} async-done(((f32[16,4,128]{2,1,0:T(4,128)}), f32[16,4,128]{2,1,0:T(4,128)S(1)}, u32[]{:S(2)}, u32[]{:S(2)}) %all-to-all-start.7) | async-done | bytes 32800 | tf_op jit(solution)/shard_map/all_to_all | solution.py:233
  137.1 18.7 %all_to_all.51.sums_ref = f32[32,4,128]{2,1,0:T(4,128)S(1)} all-to-all(f32[32,4,128]{2,1,0:T(4,128)S(1)} %shard_map.77), channel_id=1, replica_groups=mesh['y'=4,'x'=4,'z'=16,'c'=2] {'y','x','c'}, dimensions={0} | all-to-all | bytes 131072 | tf_op jit(solution)/shard_map/all_to_all | solution.py:233
  155.8 0.7 shard_map.78
  (4 shorter events, 0.1 us)
Async XLA Ops:
  12.3 21.7 %all-to-all-start = ((bf16[16,32,128]{2,1,0:T(8,128)(2,1)}), bf16[16,32,128]{2,1,0:T(8,128)(2,1)S(1)}, u32[]{:S(2)}, u32[]{:S(2)}) async-start(bf16[16,32,128]{2,1,0:T(8,128)(2,1)} %bitcast.4), calls=%async_computation | async-start | bytes 262144 | tf_op jit(solution)/shard_map/all_to_all | solution.py:233
  21.9 25.7 %collective-permute-start = (bf16[512,512]{1,0:T(8,128)(2,1)S(1)}, bf16[512,512]{1,0:T(8,128)(2,1)S(1)}, u32[]{:S(2)}, u32[]{:S(2)}) collective-permute-start(bf16[512,512]{1,0:T(8,128)(2,1)S(1)} %get-tuple-element.28.own_near), channel_id=1, source_target_pairs={{0,1},{1,0},{2,3},{3,2},{4,5},{5,4},{6,7},{7,6},{8,9},{9,8},{10,11... | collective-permute-start | bytes 1572872 | tf_op jit(solution)/shard_map/ppermute | solution.py:265
  24.4 23.1 %collective-permute-start.1 = (bf16[512,512]{1,0:T(8,128)(2,1)S(1)}, bf16[512,512]{1,0:T(8,128)(2,1)S(1)}, u32[]{:S(2)}, u32[]{:S(2)}) collective-permute-start(bf16[512,512]{1,0:T(8,128)(2,1)S(1)} %get-tuple-element.29.own_far), channel_id=1, source_target_pairs={{0,1},{1,0},{2,3},{3,2},{4,5},{5,4},{6,7},{7,6},{8,9},{9,8},{10,11... | collective-permute-start | bytes 1572872 | tf_op jit(solution)/shard_map/ppermute | solution.py:265
  121.4 15.6 %all-to-all-start.7 = ((f32[16,4,128]{2,1,0:T(4,128)}), f32[16,4,128]{2,1,0:T(4,128)S(1)}, u32[]{:S(2)}, u32[]{:S(2)}) async-start(f32[16,4,128]{2,1,0:T(4,128)} %get-tuple-element.38), calls=%async_computation.7 | async-start | bytes 65536 | tf_op jit(solution)/shard_map/all_to_all | solution.py:233
  125.5 9.9 %collective-permute-start.2 = (f32[32,128]{1,0:T(8,128)S(1)}, f32[32,128]{1,0:T(8,128)S(1)}, u32[]{:S(2)}, u32[]{:S(2)}) collective-permute-start(f32[32,128]{1,0:T(8,128)S(1)} %get-tuple-element.39), channel_id=1, source_target_pairs={{0,1},{1,0},{2,3},{3,2},{4,5},{5,4},{6,7},{7,6},{8,9},{9,8},{10,11... | collective-permute-start | bytes 49160 | tf_op jit(solution)/shard_map/ppermute | solution.py:292

commit v9 on v8

--- a/solution.py
+++ b/solution.py
@@ -67,17 +67,17 @@
     for chunk in range(CHUNKS):
         part = pl.ds(chunk * step, step)
         tile_copies.append(pltpu.make_async_copy(tiles_hbm.at[part], tiles_ref.at[part], tile_sems.at[chunk]))
-    for copy in reversed(tile_copies):
-        copy.start()
+    total = total_ref[0, 0]
+    for chunk in reversed(range(CHUNKS)):
+        pl.when(chunk * step < total)(tile_copies[chunk].start)
     for block_ref in (near_ref, far_ref):
         block_ref[...] = jnp.zeros_like(block_ref)
 
     roots_copy.wait()
     first_values(row_block, roots_ref, values_ref, hop_ref, kept_ref)
     pos_copy.wait()
-    total = total_ref[0, 0]
     row_tiles, column_tiles = near_ref.shape[0] // (2 * PV), near_ref.shape[1] // TILE
-    for chunk in reversed(range(CHUNKS)):
+    def place(chunk):
         tile_copies[chunk].wait()
         for slot in reversed(range(chunk * step, (chunk + 1) * step)):
             dest = jnp.minimum(pos_ref[0, slot], row_tiles - 1)
@@ -90,6 +90,9 @@
                     rows = pl.multiple_of(dest * 2 * PV + part * PV, PV)
                     tile = tiles_ref[slot, pl.ds(first, PV), :]
                     block_ref[pl.ds(rows, PV), lanes] = jnp.where(used, tile, jnp.zeros_like(tile))
+
+    for chunk in reversed(range(CHUNKS)):
+        pl.when(chunk * step < total)(functools.partial(place, chunk))
 
     first_products(values_ref, near_ref, far_ref, mine_ref, theirs_ref)
 

time: 157 us -> 157 us (level)
  no operation moved by 1% of the time
where the time goes in v9:
time: 157 us; the launch traced here: 156 us
  blocking collectives  112 us (71%)
  starting transfers between devices  27 us (17%)
  waiting for transfers between devices  10.1 us (6%)
  Pallas kernels  6.2 us (4%)
    all_to_all x7, blocking collectives, exchanged(): return lax.all_to_all(value, axis, 0, 0, tiled=True)  103 us
    all_to_all x2, starting transfers between devices, exchanged(): return lax.all_to_all(value, axis, 0, 0, tiled=True)  13.4 us
    all_to_all x2, waiting for transfers between devices, exchanged(): return lax.all_to_all(value, axis, 0, 0, tiled=True)  9.29 us
    ppermute x1, starting transfers between devices, local(): theirs = lax.ppermute(theirs, C, swap)  9.12 us
    all_gather x1, blocking collectives, local(): both = lax.all_gather(theirs, C)  8.77 us
    pallas_call x12, Pallas kernels, call(): pl.pallas_call(kernel, out_shape=out_shape, in_specs=in_specs, out_specs=...  6.2 us
  transfers between devices with their start and end apart: 5, of which 3 were waited for; matrix products, arithmetic and copies ran while one was open for 0% of the time, Pallas kernels for 0%

profile of v9, /device:TPU:1, one launch (start us, length us, event | category | flops | bytes accessed | tf_op | source)
XLA Modules:
  0.0 156.3 jit_solution(2594481857020518237)
XLA Ops:
  1.3 1.6 %shard_map.67 = (bf16[512,512]{1,0:T(8,128)(2,1)S(1)}, bf16[512,512]{1,0:T(8,128)(2,1)S(1)}, bf16[512,128]{1,0:T(8,128)(2,1)S(1)}, bf16[512,128]{1,0:T(8,128)(2,...) custom-call(s32[1,1]{1,0:T(1,128)S(6)} %copy.7.total_ref, s32[2,32]{1,0:T(2,128)} %bitcast.20, ...), custom_call_target="tpu_custom_call" | custom-call | tf_op jit(solution)/shard_map/pallas_call | solution.py:29
  2.9 8.8 %all-gather = bf16[1024,128]{1,0:T(8,128)(2,1)S(1)} all-gather(bf16[512,128]{1,0:T(8,128)(2,1)S(1)} %get-tuple-element.24), channel_id=2, replica_groups=mesh['y'=4,'x'=4,'z'=16,'c'=2] {'c'}, dimensions={0}, use_global_device_ids=true | all-gather | bytes 393216 | tf_op jit(solution)/shard_map/all_gather | solution.py:267
  11.7 0.7 shard_map.68
  12.3 9.4 %all-to-all-start = ((bf16[16,32,128]{2,1,0:T(8,128)(2,1)}), bf16[16,32,128]{2,1,0:T(8,128)(2,1)S(1)}, u32[]{:S(2)}, u32[]{:S(2)}) async-start(bf16[16,32,128]{2,1,0:T(8,128)(2,1)} %bitcast.4), calls=%async_computation | async-start | bytes 262144 | tf_op jit(solution)/shard_map/all_to_all | solution.py:236
  21.7 2.6 %collective-permute-start = (bf16[512,512]{1,0:T(8,128)(2,1)S(1)}, bf16[512,512]{1,0:T(8,128)(2,1)S(1)}, u32[]{:S(2)}, u32[]{:S(2)}) collective-permute-start(bf16[512,512]{1,0:T(8,128)(2,1)S(1)} %get-tuple-element.28.own_near), channel_id=1, source_target_pairs={{0,1},{1,0},{2,3},{3,2},{4,5},{5,4},{6,7},{7,6},{8,9},{9,8},{10,11... | collective-permute-start | bytes 1572872 | tf_op jit(solution)/shard_map/ppermute | solution.py:268
  24.3 1.9 %collective-permute-start.1 = (bf16[512,512]{1,0:T(8,128)(2,1)S(1)}, bf16[512,512]{1,0:T(8,128)(2,1)S(1)}, u32[]{:S(2)}, u32[]{:S(2)}) collective-permute-start(bf16[512,512]{1,0:T(8,128)(2,1)S(1)} %get-tuple-element.29.own_far), channel_id=1, source_target_pairs={{0,1},{1,0},{2,3},{3,2},{4,5},{5,4},{6,7},{7,6},{8,9},{9,8},{10,11... | collective-permute-start | bytes 1572872 | tf_op jit(solution)/shard_map/ppermute | solution.py:268
  26.2 7.7 %all-to-all-done.parts_ref = bf16[16,32,128]{2,1,0:T(8,128)(2,1)S(1)} async-done(((bf16[16,32,128]{2,1,0:T(8,128)(2,1)}), bf16[16,32,128]{2,1,0:T(8,128)(2,1)S(1)}, u32[]{:S(2)}, u32[]{:S(2)}) %all-to-all-start) | async-done | bytes 131104 | tf_op jit(solution)/shard_map/all_to_all | solution.py:236
  33.9 13.3 %all_to_all.45 = bf16[16,32,128]{2,1,0:T(8,128)(2,1)S(1)} all-to-all(bf16[16,32,128]{2,1,0:T(8,128)(2,1)S(1)} %get-tuple-element.27), channel_id=1, replica_groups=mesh['y'=4,'x'=4,'z'=16,'c'=2] {'y','x'}, dimensions={0} | all-to-all | bytes 262144 | tf_op jit(solution)/shard_map/all_to_all | solution.py:236
  47.2 0.1 shard_map.70.turned_ref
  47.3 0.0 collective-permute-done.other_near
  47.3 0.0 collective-permute-done.1.other_far
  47.3 0.7 shard_map.71
  48.1 18.2 %all_to_all.46.parts_ref = bf16[16,32,128]{2,1,0:T(8,128)(2,1)S(1)} all-to-all(bf16[16,32,128]{2,1,0:T(8,128)(2,1)S(1)} %bitcast.16), channel_id=1, replica_groups=mesh['y'=4,'x'=4,'z'=16,'c'=2] {'z'}, dimensions={0} | all-to-all | bytes 262144 | tf_op jit(solution)/shard_map/all_to_all | solution.py:236
  66.3 9.9 %all_to_all.47 = bf16[16,32,128]{2,1,0:T(8,128)(2,1)S(1)} all-to-all(bf16[16,32,128]{2,1,0:T(8,128)(2,1)S(1)} %get-tuple-element.32), channel_id=1, replica_groups=mesh['y'=4,'x'=4,'z'=16,'c'=2] {'y','x'}, dimensions={0} | all-to-all | bytes 262144 | tf_op jit(solution)/shard_map/all_to_all | solution.py:236
  76.3 0.8 shard_map.73
  77.0 16.9 %all_to_all.48.parts_ref = bf16[16,32,128]{2,1,0:T(8,128)(2,1)S(1)} all-to-all(bf16[16,32,128]{2,1,0:T(8,128)(2,1)S(1)} %bitcast.18), channel_id=1, replica_groups=mesh['y'=4,'x'=4,'z'=16,'c'=2] {'z'}, dimensions={0} | all-to-all | bytes 262144 | tf_op jit(solution)/shard_map/all_to_all | solution.py:236
  94.0 9.9 %all_to_all.49 = bf16[16,32,128]{2,1,0:T(8,128)(2,1)S(1)} all-to-all(bf16[16,32,128]{2,1,0:T(8,128)(2,1)S(1)} %get-tuple-element.35), channel_id=1, replica_groups=mesh['y'=4,'x'=4,'z'=16,'c'=2] {'y','x'}, dimensions={0} | all-to-all | bytes 262144 | tf_op jit(solution)/shard_map/all_to_all | solution.py:236
  103.9 0.8 shard_map.75
  104.7 15.8 %all_to_all.50.parts_ref = bf16[16,32,128]{2,1,0:T(8,128)(2,1)S(1)} all-to-all(bf16[16,32,128]{2,1,0:T(8,128)(2,1)S(1)} %bitcast.15), channel_id=1, replica_groups=mesh['y'=4,'x'=4,'z'=16,'c'=2] {'z'}, dimensions={0} | all-to-all | bytes 262144 | tf_op jit(solution)/shard_map/all_to_all | solution.py:236
  120.5 0.7 shard_map.76
  121.2 4.0 %all-to-all-start.7 = ((f32[16,4,128]{2,1,0:T(4,128)}), f32[16,4,128]{2,1,0:T(4,128)S(1)}, u32[]{:S(2)}, u32[]{:S(2)}) async-start(f32[16,4,128]{2,1,0:T(4,128)} %get-tuple-element.38), calls=%async_computation.7 | async-start | bytes 65536 | tf_op jit(solution)/shard_map/all_to_all | solution.py:236
  125.3 9.1 %collective-permute-start.2 = (f32[32,128]{1,0:T(8,128)S(1)}, f32[32,128]{1,0:T(8,128)S(1)}, u32[]{:S(2)}, u32[]{:S(2)}) collective-permute-start(f32[32,128]{1,0:T(8,128)S(1)} %get-tuple-element.39), channel_id=1, source_target_pairs={{0,1},{1,0},{2,3},{3,2},{4,5},{5,4},{6,7},{7,6},{8,9},{9,8},{10,11... | collective-permute-start | bytes 49160 | tf_op jit(solution)/shard_map/ppermute | solution.py:295
  134.4 0.8 collective-permute-done.2.theirs_ref
  135.2 1.6 %all-to-all-done.7.parts_ref = f32[16,4,128]{2,1,0:T(4,128)S(1)} async-done(((f32[16,4,128]{2,1,0:T(4,128)}), f32[16,4,128]{2,1,0:T(4,128)S(1)}, u32[]{:S(2)}, u32[]{:S(2)}) %all-to-all-start.7) | async-done | bytes 32800 | tf_op jit(solution)/shard_map/all_to_all | solution.py:236
  136.9 18.7 %all_to_all.51.sums_ref = f32[32,4,128]{2,1,0:T(4,128)S(1)} all-to-all(f32[32,4,128]{2,1,0:T(4,128)S(1)} %shard_map.77), channel_id=1, replica_groups=mesh['y'=4,'x'=4,'z'=16,'c'=2] {'y','x','c'}, dimensions={0} | all-to-all | bytes 131072 | tf_op jit(solution)/shard_map/all_to_all | solution.py:236
  155.6 0.7 shard_map.78
  (4 shorter events, 0.1 us)
Async XLA Ops:
  12.3 21.5 %all-to-all-start = ((bf16[16,32,128]{2,1,0:T(8,128)(2,1)}), bf16[16,32,128]{2,1,0:T(8,128)(2,1)S(1)}, u32[]{:S(2)}, u32[]{:S(2)}) async-start(bf16[16,32,128]{2,1,0:T(8,128)(2,1)} %bitcast.4), calls=%async_computation | async-start | bytes 262144 | tf_op jit(solution)/shard_map/all_to_all | solution.py:236
  21.7 25.6 %collective-permute-start = (bf16[512,512]{1,0:T(8,128)(2,1)S(1)}, bf16[512,512]{1,0:T(8,128)(2,1)S(1)}, u32[]{:S(2)}, u32[]{:S(2)}) collective-permute-start(bf16[512,512]{1,0:T(8,128)(2,1)S(1)} %get-tuple-element.28.own_near), channel_id=1, source_target_pairs={{0,1},{1,0},{2,3},{3,2},{4,5},{5,4},{6,7},{7,6},{8,9},{9,8},{10,11... | collective-permute-start | bytes 1572872 | tf_op jit(solution)/shard_map/ppermute | solution.py:268
  24.3 23.0 %collective-permute-start.1 = (bf16[512,512]{1,0:T(8,128)(2,1)S(1)}, bf16[512,512]{1,0:T(8,128)(2,1)S(1)}, u32[]{:S(2)}, u32[]{:S(2)}) collective-permute-start(bf16[512,512]{1,0:T(8,128)(2,1)S(1)} %get-tuple-element.29.own_far), channel_id=1, source_target_pairs={{0,1},{1,0},{2,3},{3,2},{4,5},{5,4},{6,7},{7,6},{8,9},{9,8},{10,11... | collective-permute-start | bytes 1572872 | tf_op jit(solution)/shard_map/ppermute | solution.py:268
  121.2 15.6 %all-to-all-start.7 = ((f32[16,4,128]{2,1,0:T(4,128)}), f32[16,4,128]{2,1,0:T(4,128)S(1)}, u32[]{:S(2)}, u32[]{:S(2)}) async-start(f32[16,4,128]{2,1,0:T(4,128)} %get-tuple-element.38), calls=%async_computation.7 | async-start | bytes 65536 | tf_op jit(solution)/shard_map/all_to_all | solution.py:236
  125.3 9.9 %collective-permute-start.2 = (f32[32,128]{1,0:T(8,128)S(1)}, f32[32,128]{1,0:T(8,128)S(1)}, u32[]{:S(2)}, u32[]{:S(2)}) collective-permute-start(f32[32,128]{1,0:T(8,128)S(1)} %get-tuple-element.39), channel_id=1, source_target_pairs={{0,1},{1,0},{2,3},{3,2},{4,5},{5,4},{6,7},{7,6},{8,9},{9,8},{10,11... | collective-permute-start | bytes 49160 | tf_op jit(solution)/shard_map/ppermute | solution.py:295
